TPU v7x, 128 devices: a whole 4x4x4 slice. The times are simulated.
128 devices in a mesh: tp: 16 (over x, z_lo, core), dp: 8 (over y, z_hi).
Axes of the slice: x: 4, y: 4, z: 4 (z_hi: 2, z_lo: 2; z = z_hi * 2 + z_lo), core: 2. Of those that a mesh axis runs over, the one named last changes fastest.
Arguments:
- tokens: bfloat16 [8192, 8192], P(('dp', 'tp')), parts along dimension 0, may hold values from -8 to 8
- gain_attn: bfloat16 [8192], replicated, may hold values from 0.099609375 to 1.8984375
- w_query: bfloat16 [8192, 8192], P(None, 'tp')
- w_key: bfloat16 [8192, 1024], P(None, 'tp')
- w_value: bfloat16 [8192, 1024], P(None, 'tp'), may hold values from -0.0625 to 0.0625
- w_out: bfloat16 [8192, 8192], P('tp'), may hold values from -0.1875 to 0.1875
- gain_mlp: bfloat16 [8192], replicated, may hold values from 0.099609375 to 1.8984375
Outputs:
- stream: bfloat16 [8192, 8192], P(('dp', 'tp')), parts along dimension 0
- mlp_input: bfloat16 [8192, 8192], P(('dp', 'tp')), parts along dimension 0
There are 8 independent parts, one for each index of `dp`. A program takes and returns all parts, laid end to end along the dimension named above; an argument that names none is the same for every part. Nothing has to cross between parts.
All inputs are finite; a program needn't handle non-finite values.
Results may differ from a plain program's by a relative error of at most 0.024.
Values may be sent and summed in bfloat16 or wider, within the bound.
A program may use at most 128 MiB of HBM per device.

v0:
```python
import math

import jax
import jax.numpy as jnp
from jax import lax
from jax.sharding import PartitionSpec as P

HD = 128


def swapped(value, axis, distance):
    mask = 2**distance
    pairs = [(source, source ^ mask) for source in range(lax.axis_size(axis))]
    return lax.ppermute(value, axis, pairs)


def rms_scaled(rows_in, gain):
    as_float = rows_in.astype(jnp.float32)
    inv_rms = lax.rsqrt(jnp.mean(as_float * as_float, axis=-1, keepdims=True) + 1e-05)
    return as_float * inv_rms * gain.astype(jnp.float32)


def rotary(as_float, positions, col_start):
    row_count, col_count = as_float.shape
    paired = as_float.reshape(row_count, col_count // 2, 2)
    pair_index = (col_start // 2 + jnp.arange(col_count // 2, dtype=jnp.int32)) % (HD // 2)
    inverse = jnp.exp(pair_index.astype(jnp.float32) * (-2.0 * math.log(500000.0) / HD))
    angles = positions[:, None] * inverse[None, :]
    cos_part = jnp.cos(angles)
    sine_part = jnp.sin(angles)
    even_part = paired[..., 0]
    odd_part = paired[..., 1]
    turned = jnp.stack(
        [even_part * cos_part - odd_part * sine_part, even_part * sine_part + odd_part * cos_part],
        axis=-1,
    )
    return turned.reshape(row_count, col_count)


def attend(query_heads, key_heads, value_heads):
    row_count = query_heads.shape[0]
    scores = jnp.einsum(
        "qhd,khd->hqk", query_heads, key_heads, preferred_element_type=jnp.float32
    ) * HD ** (-0.5)
    visible = jnp.arange(row_count)[:, None] >= jnp.arange(row_count)[None, :]
    scores = jnp.where(visible[None, :, :], scores, -1e30)
    row_top = jnp.max(scores, axis=-1, keepdims=True)
    soft_weights = jnp.exp(scores - row_top)
    probs = (soft_weights / jnp.sum(soft_weights, axis=-1, keepdims=True)).astype(jnp.bfloat16)
    context = jnp.einsum("hqk,khd->qhd", probs, value_heads, preferred_element_type=jnp.float32)
    return context.astype(jnp.bfloat16).reshape(row_count, -1)


def shards(tokens, gain_attn, w_query, w_key, w_value, w_out, gain_mlp):
    own_rows = tokens.shape[0]
    tp_place = lax.axis_index("tp")
    query_cols = w_query.shape[1]
    key_cols = w_key.shape[1]
    normed_rows = rms_scaled(lax.all_gather(tokens, "tp", axis=0, tiled=True), gain_attn).astype(
        jnp.bfloat16
    )
    joined_rows = jnp.concatenate(
        [
            jnp.dot(normed_rows, w_query, preferred_element_type=jnp.float32),
            jnp.dot(normed_rows, w_key, preferred_element_type=jnp.float32),
            jnp.dot(normed_rows, w_value, preferred_element_type=jnp.float32),
        ],
        axis=1,
    )
    total_rows = joined_rows.shape[0]
    positions = jnp.arange(total_rows, dtype=jnp.int32).astype(jnp.float32)
    query_part = rotary(joined_rows[:, :query_cols], positions, tp_place * query_cols).astype(
        jnp.bfloat16
    )
    key_part = rotary(
        joined_rows[:, query_cols : query_cols + key_cols], positions, tp_place * key_cols
    ).astype(jnp.bfloat16)
    value_part = joined_rows[:, query_cols + key_cols :].astype(jnp.bfloat16)
    other_key, other_value = swapped((key_part, value_part), "tp", 0)
    lower_half = tp_place % 2 == 0
    key_part = jnp.where(
        lower_half,
        jnp.concatenate([key_part, other_key], axis=1),
        jnp.concatenate([other_key, key_part], axis=1),
    )
    value_part = jnp.where(
        lower_half,
        jnp.concatenate([value_part, other_value], axis=1),
        jnp.concatenate([other_value, value_part], axis=1),
    )
    local_heads = query_cols // HD
    key_heads = jnp.broadcast_to(key_part.reshape(total_rows, 1, HD), (total_rows, local_heads, HD))
    value_heads = jnp.broadcast_to(
        value_part.reshape(total_rows, 1, HD), (total_rows, local_heads, HD)
    )
    context = attend(query_part.reshape(total_rows, local_heads, HD), key_heads, value_heads)
    summed = lax.psum(
        jnp.dot(context, w_out, preferred_element_type=jnp.float32).astype(jnp.bfloat16), "tp"
    ).astype(jnp.float32)
    head_sum = lax.dynamic_slice_in_dim(summed, tp_place * own_rows, own_rows, 0)
    stream = (tokens.astype(jnp.float32) + head_sum).astype(jnp.bfloat16)
    stream = lax.optimization_barrier(stream)
    mlp_input = rms_scaled(stream, gain_mlp).astype(jnp.bfloat16)
    return (stream, mlp_input)


def solution(mesh):
    placed = (
        P(("dp", "tp"), None),
        P(),
        P(None, "tp"),
        P(None, "tp"),
        P(None, "tp"),
        P("tp", None),
        P(),
    )
    return jax.shard_map(
        shards,
        mesh=mesh,
        in_specs=placed,
        out_specs=(P(("dp", "tp"), None), P(("dp", "tp"), None)),
        check_vma=False,
    )
```

profile of v0, /device:TPU:1, one launch (start us, length us, event | category | flops | bytes accessed | tf_op | source)
XLA Modules:
  0.0 586.0 jit_solution(4155088736511624577)
XLA Ops:
  7.2 0.7 all-gather.2.cloned.1.call-update
  8.0 0.7 convert_element_type.79
  8.7 1.3 iota_compare_fusion
  10.0 95.0 %all-gather.2.cloned.1.call-done = bf16[1024,8192]{1,0:T(8,128)(2,1)} async-done(((bf16[64,8192]{1,0:T(8,128)(2,1)}), bf16[1024,8192]{1,0:T(8,128)(2,1)}) %all-gather.2.cloned.1.call-update) | async-done | bytes 16777232 | tf_op jit(solution)/shard_map/all_gather | solution.py:59
  105.1 7.2 %fusion.1 = f32[1024]{0:T(1024)S(1)} fusion(bf16[1024,8192]{1,0:T(8,128)(2,1)} %all-gather.2.cloned.1.call-done), kind=kLoop, calls=%fused_computation.3 | loop fusion | flops 25164800 | bytes 16781312 | tf_op jit(solution)/shard_map/reduce_sum | solution.py:19
  112.3 9.8 %fusion.3 = bf16[1024,8192]{1,0:T(8,128)(2,1)S(1)} fusion(bf16[1024,8192]{1,0:T(8,128)(2,1)} %all-gather.2.cloned.1.call-done, f32[8192]{0:T(1024)S(1)} %convert_element_type.79, f32[1024]{0:T(1024)S(1)} %add_rsqrt_fusion), kind=kLoop, calls=%fused_computation.5 | loop fusion | flops 33554432 | bytes 33591296 | tf_op jit(solution)/shard_map/convert_element_type | solution.py:59
  122.1 5.7 copy-done.2
  127.8 5.2 fusion.57
  133.0 0.1 reshape.329
  133.1 0.2 fusion.50
  133.4 0.6 fusion.36
  134.0 0.1 copy.23
  134.2 0.3 collective-permute-start.1
  134.5 10.9 %convolution_convert_fusion.1 = bf16[1024,64]{0,1:T(8,128)(2,1)S(1)} fusion(bf16[1024,8192]{1,0:T(8,128)(2,1)} %copy-done.2, bf16[8192,64]{0,1:T(8,128)(2,1)S(1)} %copy-done.5), kind=kOutput, calls=%fused_computation.30 | convolution fusion | flops 1073807360 | bytes 17956864 | tf_op jit(solution)/shard_map/dot_general | solution.py:66
  145.4 0.5 collective-permute-start
  146.0 15.8 %fusion.56 = f32[1024,512]{0,1:T(8,128)} fusion(bf16[1024,8192]{1,0:T(8,128)(2,1)} %copy-done.2, bf16[8192,512]{1,0:T(8,128)(2,1)} %param.9), kind=kOutput, calls=%fused_computation.75 | convolution fusion | flops 8589934592 | bytes 27262976 | tf_op jit(solution)/shard_map/dot_general | solution.py:64
  161.8 2.5 reshape.328
  164.3 2.9 fusion.49
  167.2 2.3 copy.31
  169.6 2.3 copy.32
  171.9 4.7 fusion.20
  176.7 1.1 copy.20
  177.9 0.4 convert_element_type.84
  178.3 1.1 maximum_select_fusion
  179.5 0.2 copy.24
  179.6 10.6 %fusion.51 = (f32[4,1024]{1,0:T(4,128)S(1)}, f32[4,1024,1024]{1,2,0:T(8,128)}) fusion(pred[1024,1024]{0,1:T(8,128)(4,1)} %iota_compare_fusion, bf16[1024,4,128]{0,2,1:T(8,128)(2,1)S(1)} %convert_element_type.84, bf16[1024,128]{1,0:T(8,128)(2,1)S(1)} %copy.24), kind=kOutput, calls=%fused_computation.74 | convolution fusion | flops 1090520064 | bytes 19152896 | tf_op jit(solution)/shard_map/sub | solution.py:48
  190.3 7.1 %fusion.14 = bf16[4,128,1024]{2,1,0:T(8,128)(2,1)S(1)} fusion(f32[4,1024,1024]{1,2,0:T(8,128)} %get-tuple-element.11, f32[4,1024]{1,0:T(4,128)S(1)} %get-tuple-element.10, bf16[1024,128]{0,1:T(8,128)(2,1)S(1)} %get-tuple-element.12), kind=kOutput, calls=%fused_computation.25 | convolution fusion | flops 1082654720 | bytes 18104320 | tf_op jit(solution)/shard_map/hqk,khd->qhd/dot_general | solution.py:50
  197.3 15.9 %convolution_convert_fusion = bf16[1024,8192]{1,0:T(8,128)(2,1)} fusion(bf16[1024,512]{0,1:T(8,128)(2,1)S(1)} %bitcast.21, bf16[512,8192]{1,0:T(8,128)(2,1)} %param.12), kind=kOutput, calls=%fused_computation.9 | convolution fusion | flops 8598323200 | bytes 26214400 | tf_op jit(solution)/shard_map/dot_general | solution.py:98
  213.3 362.7 %all-reduce.2.cloned.1.call-done = bf16[1024,8192]{1,0:T(8,128)(2,1)} async-done(((bf16[1024,8192]{1,0:T(8,128)(2,1)}), bf16[1024,8192]{1,0:T(8,128)(2,1)}) %all-reduce.2.cloned.1.call-update) | async-done | bytes 16777232 | tf_op jit(solution)/shard_map/psum | solution.py:97
  576.0 1.5 add_convert_fusion
  577.5 0.3 fusion.9
  577.8 1.3 fusion.11
  (27 shorter events, 0.4 us)
Async XLA Ops:
  7.2 120.6 %copy-start = (bf16[8192,64]{0,1:T(8,128)(2,1)S(1)}, bf16[8192,64]{0,1:T(8,128)(2,1)}, u32[]{:S(2)}) copy-start(bf16[8192,64]{0,1:T(8,128)(2,1)} %param.10) | copy-start | bytes 3145732
  7.2 97.9 %all-gather.2.cloned.1.call-start = ((), (), s32[]{:S(2)}) async-start(), calls=%async_computation | async-start | bytes 17825792 | tf_op jit(solution)/shard_map/all_gather | solution.py:59
  7.9 568.1 %all-reduce.2.cloned.1.call-start = ((), (), s32[]{:S(2)}) async-start(), calls=%async_computation.1 | async-start | bytes 33554432 | tf_op jit(solution)/shard_map/psum | solution.py:97
  122.1 5.7 copy-start.2
  127.8 6.7 %copy-start.5 = (bf16[8192,64]{0,1:T(8,128)(2,1)S(1)}, bf16[8192,64]{0,1:T(8,128)(2,1)}, u32[]{:S(2)}) copy-start(bf16[8192,64]{0,1:T(8,128)(2,1)} %param.11) | copy-start | bytes 3145732
  134.2 44.2 %collective-permute-start.1 = (bf16[1024,64]{0,1:T(8,128)(2,1)S(1)}, bf16[1024,64]{0,1:T(8,128)(2,1)S(1)}, u32[]{:S(2)}, u32[]{:S(2)}) collective-permute-start(bf16[1024,64]{0,1:T(8,128)(2,1)S(1)} %convert_element_type.86), channel_id=1, source_target_pairs={{0,8},{8,0},{16,24},{24,16},{32,40},{40,32},{48,56},{56,48},{64,72... | collective-permute-start | bytes 393224 | tf_op jit(solution)/shard_map/ppermute | solution.py:14
  145.4 32.9 %collective-permute-start = (bf16[1024,64]{0,1:T(8,128)(2,1)S(1)}, bf16[1024,64]{0,1:T(8,128)(2,1)}, u32[]{:S(2)}, u32[]{:S(2)}) collective-permute-start(bf16[1024,64]{0,1:T(8,128)(2,1)S(1)} %convolution_convert_fusion.1), channel_id=1, source_target_pairs={{0,8},{8,0},{16,24},{24,16},{32,40},{40,32},{48,56},{56,48},{64,72... | collective-permute-start | bytes 393224 | tf_op jit(solution)/shard_map/ppermute | solution.py:14
  197.3 16.0 %copy-start.6 = (bf16[8192]{0:T(1024)(128)(2,1)S(1)}, bf16[8192]{0:T(1024)(128)(2,1)}, u32[]{:S(2)}) copy-start(bf16[8192]{0:T(1024)(128)(2,1)} %param.13) | copy-start | bytes 49156
  197.3 378.7 %copy-start.4 = (bf16[64,8192]{1,0:T(8,128)(2,1)S(1)}, bf16[64,8192]{1,0:T(8,128)(2,1)}, u32[]{:S(2)}) copy-start(bf16[64,8192]{1,0:T(8,128)(2,1)} %param.7) | copy-start | bytes 3145732
  197.3 381.8 %copy-start.1 = (bf16[8192,64]{0,1:T(8,128)(2,1)S(1)}, bf16[8192,64]{0,1:T(8,128)(2,1)}, u32[]{:S(2)}) copy-start(bf16[8192,64]{0,1:T(8,128)(2,1)} %param.10) | copy-start | bytes 3145732
  577.5 1.6 copy-start.3
Sparse Core Ops, SparseCore 0:
  9.7 95.2 all-gather.1
  213.4 362.5 all-reduce.1
where the time goes:
time: 586 us
  waiting for transfers between devices  458 us (78%)
  matrix products  65.6 us (11%)
  other arithmetic  28.6 us (5%)
  local copies, waits for them, and re-layouts  18.1 us (3%)
  between operations  14.3 us (2%)
    psum x1, waiting for transfers between devices, shards(): lax.psum(jnp.dot(context, w_out, preferred_element_type=jnp.float32).asty...  363 us
    all_gather x1, waiting for transfers between devices, shards(): lax.all_gather(tokens, 'tp', axis=0, tiled=True)  95 us
    dot_general x1, matrix products, shards(): jnp.dot(context, w_out, preferred_element_type=jnp.float32)  15.9 us
    dot_general x1, matrix products, shards(): jnp.dot(normed_rows, w_query, preferred_element_type=jnp.float32)  15.8 us
  transfers between devices with their start and end apart: 4, of which 2 were waited for; matrix products, arithmetic and copies ran while one was open for 8% of the time, Pallas kernels for 0%

commit v1 on v0

v1 whole, which is shorter than its diff:
```python
import math

import jax
import jax.numpy as jnp
import numpy as np
from jax import lax
from jax.experimental import pallas as pl
from jax.experimental.pallas import tpu as pltpu
from jax.sharding import PartitionSpec as P

MESH = pl.DeviceIdType.MESH
BF16 = jnp.bfloat16
F32 = jnp.float32
D = 8192
HD = 128
NX = 4
BLK = 256
PIECE = 2048
NQ = D // PIECE
HEADS = 4
WCH = 1024


def rotary_tables():
    inverse = np.exp(np.arange(HD // 2) * (-2.0 * math.log(500000.0) / HD))
    angles = np.arange(NX * BLK)[:, None] * inverse[None, :]
    cos = np.repeat(np.cos(angles), 2, axis=1).astype(np.float32)
    sin = np.repeat(np.sin(angles), 2, axis=1)
    sin[:, 0::2] *= -1.0
    return cos, sin.astype(np.float32)


def kernel(
    tok_hbm, gain_attn, wq_hbm, wk_hbm, wv_hbm, wo_hbm, gain_mlp, cos_hbm, sin_hbm,
    stream_hbm, mlp_hbm,
    xs, wq, wkv, wkst, wvst, wo, qb, kvl, kvr, ctx, ctxr, acc, cos, sin, bias, rz, rr, rx, tok,
    s_in, s_wst, s_send, s_xr, s_zr, s_sib, s_w, s_kvs, s_kvr, s_ctx, s_rsend, s_rz, s_rr, s_rx, s_out,
):
    tp, dp = lax.axis_index("tp"), lax.axis_index("dp")
    x, zl, c = tp // 4, (tp // 2) % 2, tp % 2
    y, zz = dp // 2, (dp % 2) * 2 + zl

    def device(x_to, z_to, c_to):
        return (x_to * 4 + (z_to % 2) * 2 + c_to, y * 2 + z_to // 2)

    right, left = device((x + 1) % 4, zz, c), device((x + 3) % 4, zz, c)
    above, below = device(x, (zz + 1) % 4, c), device(x, (zz + 3) % 4, c)
    across, sibling = device(x, (zz + 2) % 4, c), device(x, zz, 1 - c)
    b_own, b_right, b_far, b_left = x, (x + 1) % 4, (x + 2) % 4, (x + 3) % 4

    def remote(src, dst, send_sem, recv_sem, to):
        return pltpu.make_async_remote_copy(
            src_ref=src, dst_ref=dst, send_sem=send_sem, recv_sem=recv_sem,
            device_id=to, device_id_type=MESH,
        )

    def cols(q):
        return pl.ds(pl.multiple_of(q * PIECE, PIECE), PIECE)

    def rows(start, size):
        return pl.ds(pl.multiple_of(start, 32), size)

    tok_copy = pltpu.make_async_copy(tok_hbm, tok, s_in.at[0])
    tok_copy.start()
    barrier = pltpu.get_barrier_semaphore()
    for neighbour in (right, left, above, below, across, sibling):
        pl.semaphore_signal(barrier, inc=1, device_id=neighbour, device_id_type=MESH)

    def stage(k):
        part = pl.ds(k * WCH, WCH)
        return (
            pltpu.make_async_copy(wk_hbm.at[part], wkst.at[k % 2], s_wst.at[0, k % 2]),
            pltpu.make_async_copy(wv_hbm.at[part], wvst.at[k % 2], s_wst.at[1, k % 2]),
        )

    for k in range(2):
        for copy in stage(k):
            copy.start()
    in_copies = [
        pltpu.make_async_copy(wq_hbm, wq, s_in.at[1]),
        pltpu.make_async_copy(cos_hbm, cos, s_in.at[2]),
        pltpu.make_async_copy(sin_hbm, sin, s_in.at[3]),
        pltpu.make_async_copy(wo_hbm, wo.at[0], s_in.at[4]),
    ]
    for copy in in_copies:
        copy.start()

    tok_copy.wait()

    def norm_rows(i, carry):
        part = pl.ds(pl.multiple_of(i * 16, 16), 16)
        as_float = tok[part, :].astype(F32)
        inv = lax.rsqrt(jnp.mean(as_float * as_float, axis=-1, keepdims=True) + 1e-05)
        normed = as_float * inv * gain_attn[...].astype(F32)
        xs[x, pl.ds(pl.multiple_of(c * 64 + i * 16, 16), 16), :] = normed.astype(BF16)
        return carry

    lax.fori_loop(0, 4, norm_rows, 0)
    pl.semaphore_wait(barrier, 6)

    own_rows = rows(c * 64, 64)
    from_below = 192 - 64 * zl
    from_above = 128 + 64 * zl

    def send_x(b, q, way):
        ref = xs.at[b, own_rows, cols(q)]
        return remote(ref, ref, s_send.at[way, b], s_xr.at[b, q], (right, left)[way])

    def send_z(b, q, way):
        src = xs.at[b, rows(c * 64 + 32 * way, 32), cols(q)]
        at = (from_above, from_below)[way]
        dst = xs.at[b, rows(at + c * 32, 32), cols(q)]
        return remote(src, dst, s_send.at[2 + way, b], s_zr.at[way, b, q], (above, below)[way])

    def recv_z(b, q, way):
        at = (from_below, from_above)[way]
        ref = xs.at[b, rows(at + c * 32, 32), cols(q)]
        remote(ref, ref, s_send.at[2 + way, b], s_zr.at[way, b, q], sibling).wait_recv()

    def sib_ref(b, q, kind, core):
        if kind == 0:
            return xs.at[b, rows(core * 64, 64), cols(q)]
        at = (from_below, from_above)[kind - 1]
        return xs.at[b, rows(at + core * 32, 32), cols(q)]

    def send_sib(b, q, kind):
        ref = sib_ref(b, q, kind, c)
        remote(ref, ref, s_send.at[4 + kind, b], s_sib.at[kind, b, q], sibling).start()

    def recv_sib(b, q):
        for kind in range(3):
            ref = sib_ref(b, q, kind, 1 - c)
            remote(ref, ref, s_send.at[4 + kind, b], s_sib.at[kind, b, q], sibling).wait_recv()

    def spread(b, q):
        send_z(b, q, 0).start()
        send_z(b, q, 1).start()
        send_sib(b, q, 0)

    def start_own(q, carry):
        send_x(b_own, q, 0).start()
        send_x(b_own, q, 1).start()
        spread(b_own, q)
        return carry

    lax.fori_loop(0, NQ, start_own, 0)
    wo_send = remote(wo_hbm, wo.at[1], s_w.at[0], s_w.at[1], sibling)

    wkv_cols = pl.ds(pl.multiple_of(c * HD, HD), HD)
    for k in range(D // WCH):
        for copy in stage(k):
            copy.wait()
        joined = jnp.concatenate([wkst[k % 2], wvst[k % 2]], axis=1)
        wkv[pl.ds(k * WCH, WCH), wkv_cols] = joined
        if k + 2 < D // WCH:
            for copy in stage(k + 2):
                copy.start()
    wkv_send = remote(wkv.at[:, wkv_cols], wkv.at[:, wkv_cols], s_w.at[2], s_w.at[3], sibling)
    wkv_send.start()
    wo_send.start()

    def place(row):
        other = row >= 192
        inner = jnp.where(other, row - 192, row - 128)
        half = jnp.where(other, zl, 1 - zl)
        far = (1 - zl) * 128 + (inner // 32) * 64 + half * 32 + inner % 32
        return jnp.where(row < 128, zl * 128 + row, far)

    queries = place(lax.broadcasted_iota(jnp.int32, (BLK, BLK), 0))
    keys = place(lax.broadcasted_iota(jnp.int32, (BLK, BLK), 1))
    bias[...] = jnp.where(queries >= keys, 0.0, -1e30)
    acc[...] = jnp.zeros_like(acc)

    def qkv(a, b, q):
        held = xs[b, :, cols(q)]
        depth = cols(q)
        for n in range(2):
            part = pl.ds(n * 256, 256)
            acc[a, :, part] += jnp.dot(held, wq[depth, part], preferred_element_type=F32)
        acc[a, :, pl.ds(512, 256)] += jnp.dot(held, wkv[depth, :], preferred_element_type=F32)

    def table(ref, b):
        at = b * BLK
        far = at + (1 - zl) * 128
        parts = [ref[rows(at + zl * 128, 128), :]]
        for half in (1 - zl, zl):
            for core in range(2):
                parts.append(ref[rows(far + core * 64 + half * 32, 32), :])
        return jnp.concatenate(parts, axis=0)

    def kv_rows(b):
        return kvl.at[b, rows(c * 128, 128), :], kvr.at[b, rows(c * 128, 128), :]

    def kv_send(b):
        src, dst = kv_rows(b)
        return remote(src, dst, s_kvs.at[0, b], s_kvr.at[0, b], across)

    def kv_pass(b):
        ref = kv_rows(b)[1]
        return remote(ref, ref, s_kvs.at[1, b], s_kvr.at[1, b], sibling)

    def kv_wait(b):
        ref = kvr.at[b, rows((1 - c) * 128, 128), :]
        remote(ref, ref, s_kvs.at[1, b], s_kvr.at[1, b], sibling).wait_recv()

    def finish_qkv(a, b):
        cos_rows, sin_rows = table(cos, b), table(sin, b)
        lane = lax.broadcasted_iota(jnp.int32, (BLK, HD), 1)

        def turned(value):
            swapped = jnp.where(lane % 2 == 0, pltpu.roll(value, HD - 1, 1), pltpu.roll(value, 1, 1))
            return value * cos_rows + swapped * sin_rows

        first, second = acc[a, :, 512:640], acc[a, :, 640:768]
        key = jnp.where(lane < 64, first, pltpu.roll(second, 64, 1))
        value = jnp.where(lane < 64, pltpu.roll(first, 64, 1), second)
        kvl[b, :, 0:HD] = turned(key).astype(BF16)
        kvl[b, :, HD : 2 * HD] = value.astype(BF16)
        kv_send(b).start()
        scale = HD**-0.5 * math.log2(math.e)
        for h in range(HEADS):
            head = turned(acc[a, :, h * HD : (h + 1) * HD])
            qb[b, h] = (head * scale).astype(BF16)

    in_copies[0].wait()

    def first_loop(q, carry):
        for b, way in ((b_left, 0), (b_right, 1)):
            send_x(b, q, way).wait_recv()
            spread(b, q)

        @pl.when(q < 2)
        def _():
            send_x(b_left, q, 0).start()

        @pl.when(q >= 2)
        def _():
            send_x(b_right, q, 1).start()

        for way in range(2):
            recv_z(b_own, q, way)
            send_sib(b_own, q, 1 + way)
        recv_sib(b_own, q)

        @pl.when(q == 0)
        def _():
            remote(
                wkv.at[:, pl.ds(pl.multiple_of((1 - c) * HD, HD), HD)],
                wkv.at[:, pl.ds(pl.multiple_of((1 - c) * HD, HD), HD)],
                s_w.at[2], s_w.at[3], sibling,
            ).wait_recv()

        qkv(0, b_own, q)
        return carry

    lax.fori_loop(0, NQ, first_loop, 0)
    in_copies[1].wait()
    in_copies[2].wait()
    finish_qkv(0, b_own)
    acc[0] = jnp.zeros((BLK, 768), F32)

    def far_piece(q, way):
        send_x(b_far, q, way).wait_recv()
        spread(b_far, q)

    def second_loop(q, carry):
        for b in (b_left, b_right):
            for way in range(2):
                recv_z(b, q, way)
                send_sib(b, q, 1 + way)

        @pl.when(q == 2)
        def _():
            far_piece(0, 0)
            far_piece(2, 1)

        @pl.when(q == 3)
        def _():
            far_piece(1, 0)
            far_piece(3, 1)

        def both(a, inner):
            b = (x + 1 + 2 * a) % 4
            recv_sib(b, q)
            qkv(a, b, q)
            return inner

        lax.fori_loop(0, 2, both, 0)
        return carry

    lax.fori_loop(0, NQ, second_loop, 0)

    def finish_both(a, carry):
        finish_qkv(a, (x + 1 + 2 * a) % 4)
        return carry

    lax.fori_loop(0, 2, finish_both, 0)
    acc[0] = jnp.zeros((BLK, 768), F32)
    kv_send(b_own).wait_recv()
    kv_pass(b_own).start()

    def third_loop(i, carry):
        q = (i % 2) * 2 + i // 2
        for way in range(2):
            recv_z(b_far, q, way)
            send_sib(b_far, q, 1 + way)
        recv_sib(b_far, q)
        qkv(0, b_far, q)
        return carry

    lax.fori_loop(0, NQ, third_loop, 0)
    finish_qkv(0, b_far)

    for b in (b_right, b_left):
        kv_send(b).wait_recv()
        kv_pass(b).start()
    for b in (b_own, b_right, b_left):
        kv_wait(b)

    def scored(b, h, kb):
        q_rows = qb[b, h]
        key_in = jnp.concatenate([kvl[kb, 0:192, 0:HD], kvr[kb, 192:256, 0:HD]], axis=0)
        key_out = jnp.concatenate([kvr[kb, 0:192, 0:HD], kvl[kb, 192:256, 0:HD]], axis=0)
        dims = (((1,), (1,)), ((), ()))
        inside = lax.dot_general(q_rows[0:192], key_in, dims, preferred_element_type=F32)
        outside = lax.dot_general(q_rows[192:256], key_out, dims, preferred_element_type=F32)
        return jnp.concatenate([inside, outside], axis=0)

    def step(scores, kb, state):
        top, total, out = state
        new_top = jnp.maximum(top, jnp.max(scores, axis=-1, keepdims=True))
        weights = jnp.exp2(scores - new_top)
        fade = jnp.exp2(top - new_top)
        total = total * fade + jnp.sum(weights, axis=-1, keepdims=True)
        weights = weights.astype(BF16)
        val_in = jnp.concatenate([kvl[kb, 0:192, HD:], kvr[kb, 192:256, HD:]], axis=0)
        val_out = jnp.concatenate([kvr[kb, 0:192, HD:], kvl[kb, 192:256, HD:]], axis=0)
        inside = jnp.dot(weights[0:192], val_in, preferred_element_type=F32)
        outside = jnp.dot(weights[192:256], val_out, preferred_element_type=F32)
        return new_top, total, out * fade + jnp.concatenate([inside, outside], axis=0)

    def attend(b):
        for h in range(HEADS):
            start = (
                jnp.full((BLK, 1), -1e30, F32),
                jnp.zeros((BLK, 1), F32),
                jnp.zeros((BLK, HD), F32),
            )
            state = lax.fori_loop(0, b, lambda kb, s: step(scored(b, h, kb), kb, s), start)
            _, total, out = step(scored(b, h, b) + bias[...], b, state)
            out = (out / total).astype(BF16)
            at = pl.ds(h * HD, HD)
            for core in range(2):
                ctx[b, core, 0:64, at] = out[core * 64 : core * 64 + 64]
                ctx[b, core, 64:96, at] = out[128 + core * 32 : 160 + core * 32]
                ctx[b, core, 96:128, at] = out[192 + core * 32 : 224 + core * 32]
        ctx_send(b).start()

    def ctx_send(b):
        return remote(ctx.at[b, 1 - c], ctxr.at[b], s_ctx.at[0, b], s_ctx.at[1, b], sibling)

    def rs_z(b, q, way):
        at = (64 + 32 * zl, 96 - 32 * zl)[way]
        return remote(
            xs.at[b, rows(at, 32), cols(q)],
            rz.at[b, pl.ds(32 - 32 * way, 32), cols(q)],
            s_rsend.at[way, b], s_rz.at[way, b, q], (above, below)[way],
        )

    def rs_z_wait(b, q):
        for way in range(2):
            ref = rz.at[b, pl.ds(32 - 32 * way, 32), cols(q)]
            remote(ref, ref, s_rsend.at[way, b], s_rz.at[way, b, q], sibling).wait_recv()

    def project(b, q):
        def tile(n, carry):
            at = pl.ds(pl.multiple_of(q * PIECE + n * 512, 512), 512)
            total = jnp.dot(ctx[b, c], wo[0, :, at], preferred_element_type=F32)
            total += jnp.dot(ctxr[b], wo[1, :, at], preferred_element_type=F32)
            xs[b, 0:128, at] = total.astype(BF16)
            return carry

        lax.fori_loop(0, PIECE // 512, tile, 0)
        rs_z(b, q, 0).start()
        rs_z(b, q, 1).start()

    def drain(b, whole):
        half, quarter = xs.at[b, 0:64], xs.at[b, 0:32]
        for way in range(2):
            remote(quarter, quarter, s_send.at[2 + way, b], s_zr.at[way, b, 0], sibling).wait_send()
        for kind, ref in enumerate((half, quarter, quarter)):
            remote(ref, ref, s_send.at[4 + kind, b], s_sib.at[kind, b, 0], sibling).wait_send()
        for way in whole:
            remote(half, half, s_send.at[way, b], s_xr.at[b, 0], sibling).wait_send()

    def drain_half(b, way):
        ref = xs.at[b, 0:64, 0 : D // 2]
        remote(ref, ref, s_send.at[way, b], s_xr.at[b, 0], sibling).wait_send()

    def place_sum(b, q, relay):
        rs_z_wait(b, q)
        total = xs[b, 0:64, cols(q)].astype(F32) + rz[b, :, cols(q)].astype(F32)
        if relay:
            total += rr[:, cols(q)].astype(F32)
        xs[b, 0:64, cols(q)] = total.astype(BF16)

    def rs_relay(q, way):
        return remote(
            xs.at[b_far, 0:64, cols(q)], rr.at[:, cols(q)],
            s_rsend.at[2 + way, b_far], s_rr.at[q], (right, left)[way],
        )

    def rs_last(q, way):
        b = (b_right, b_left)[way]
        return remote(
            xs.at[b, 0:64, cols(q)], rx.at[way, :, cols(q)],
            s_rsend.at[2 + way, b], s_rx.at[way, q], (right, left)[way],
        )

    kv_send(b_far).wait_recv()
    kv_pass(b_far).start()
    kv_wait(b_far)
    attend(b_far)
    drain(b_far, ())
    in_copies[3].wait()
    remote(wo_hbm, wo.at[1], s_w.at[0], s_w.at[1], sibling).wait_recv()
    ctx_send(b_far).wait_recv()

    def far_project(i, carry):
        project(b_far, (i % 2) * 2 + i // 2)
        return carry

    lax.fori_loop(0, NQ, far_project, 0)

    def attend_both(a, carry):
        attend((x + 1 + 2 * a) % 4)
        place_sum(b_far, a, False)
        rs_relay(a, 0).start()
        place_sum(b_far, a + 2, False)
        rs_relay(a + 2, 1).start()
        return carry

    lax.fori_loop(0, 2, attend_both, 0)
    drain(b_right, ())
    drain_half(b_right, 1)
    drain(b_left, ())
    drain_half(b_left, 0)
    ctx_send(b_right).wait_recv()
    ctx_send(b_left).wait_recv()

    def project_both(q, carry):
        def one(a, inner):
            project((x + 1 + 2 * a) % 4, q)
            return inner

        return lax.fori_loop(0, 2, one, carry)

    lax.fori_loop(0, NQ, project_both, 0)
    attend(b_own)
    drain(b_own, (0, 1))
    ctx_send(b_own).wait_recv()

    def relay_wait(q):
        ref = rr.at[:, cols(q)]
        remote(ref, ref, s_rsend.at[2, b_far], s_rr.at[q], sibling).wait_recv()

    def own_project(q, carry):
        project(b_own, q)
        relay_wait(q)

        @pl.when(q < 2)
        def _():
            place_sum(b_right, q, True)
            place_sum(b_left, q, False)

        @pl.when(q >= 2)
        def _():
            place_sum(b_right, q, False)
            place_sum(b_left, q, True)

        rs_last(q, 0).start()
        rs_last(q, 1).start()
        return carry

    lax.fori_loop(0, NQ, own_project, 0)

    def last_sum(q, squares):
        rs_z_wait(b_own, q)
        for way in range(2):
            ref = rx.at[way, :, cols(q)]
            remote(ref, ref, s_rsend.at[2, b_own], s_rx.at[way, q], sibling).wait_recv()
        head_sum = xs[b_own, 0:64, cols(q)].astype(F32) + rz[b_own, :, cols(q)].astype(F32)
        head_sum += rx[0, :, cols(q)].astype(F32) + rx[1, :, cols(q)].astype(F32)
        stream = (tok[:, cols(q)].astype(F32) + head_sum).astype(BF16)
        tok[:, cols(q)] = stream
        pltpu.make_async_copy(tok.at[:, cols(q)], stream_hbm.at[:, cols(q)], s_out.at[q]).start()
        as_float = stream.astype(F32)
        return squares + jnp.sum(as_float * as_float, axis=-1, keepdims=True)

    squares = lax.fori_loop(0, NQ, last_sum, jnp.zeros((64, 1), F32))
    inv_rms = lax.rsqrt(squares * (1.0 / D) + 1e-05)

    def mlp_rows(q, carry):
        gain = gain_mlp[:, cols(q)].astype(F32)
        rr[:, cols(q)] = (tok[:, cols(q)].astype(F32) * inv_rms * gain).astype(BF16)
        pltpu.make_async_copy(rr.at[:, cols(q)], mlp_hbm.at[:, cols(q)], s_out.at[NQ + q]).start()
        return carry

    lax.fori_loop(0, NQ, mlp_rows, 0)

    for q in range(NQ):
        pltpu.make_async_copy(tok.at[:, cols(q)], stream_hbm.at[:, cols(q)], s_out.at[q]).wait()
        pltpu.make_async_copy(rr.at[:, cols(q)], mlp_hbm.at[:, cols(q)], s_out.at[NQ + q]).wait()
    wo_send.wait_send()
    wkv_send.wait_send()
    for b in range(NX):
        kv_send(b).wait_send()
        kv_pass(b).wait_send()
        ctx_send(b).wait_send()
        for way in range(2):
            ref = rz.at[b, 0:32]
            remote(ref, ref, s_rsend.at[way, b], s_rz.at[way, b, 0], sibling).wait_send()
    for way in range(2):
        ref = rr.at[:, 0 : D // 2]
        remote(ref, ref, s_rsend.at[2 + way, b_far], s_rr.at[0], sibling).wait_send()
        ref = rx.at[way]
        b = (b_right, b_left)[way]
        remote(ref, ref, s_rsend.at[2 + way, b], s_rx.at[way, 0], sibling).wait_send()


def sublayer(tokens, gain_attn, w_query, w_key, w_value, w_out, gain_mlp):
    cos, sin = rotary_tables()
    any_spec = pl.BlockSpec(memory_space=pl.ANY)
    vmem_spec = pl.BlockSpec(memory_space=pltpu.VMEM)
    dma = pltpu.SemaphoreType.DMA
    shape = jax.ShapeDtypeStruct((64, D), BF16)
    return pl.pallas_call(
        kernel,
        out_shape=(shape, shape),
        in_specs=[any_spec, vmem_spec] + [any_spec] * 4 + [vmem_spec] + [any_spec] * 2,
        out_specs=(any_spec, any_spec),
        scratch_shapes=[
            pltpu.VMEM((NX, BLK, D), BF16),
            pltpu.VMEM((D, 512), BF16),
            pltpu.VMEM((D, 256), BF16),
            pltpu.VMEM((2, WCH, 64), BF16),
            pltpu.VMEM((2, WCH, 64), BF16),
            pltpu.VMEM((2, 512, D), BF16),
            pltpu.VMEM((NX, HEADS, BLK, HD), BF16),
            pltpu.VMEM((NX, BLK, 256), BF16),
            pltpu.VMEM((NX, BLK, 256), BF16),
            pltpu.VMEM((NX, 2, 128, 512), BF16),
            pltpu.VMEM((NX, 128, 512), BF16),
            pltpu.VMEM((2, BLK, 768), F32),
            pltpu.VMEM((NX * BLK, HD), F32),
            pltpu.VMEM((NX * BLK, HD), F32),
            pltpu.VMEM((BLK, BLK), F32),
            pltpu.VMEM((NX, 64, D), BF16),
            pltpu.VMEM((64, D), BF16),
            pltpu.VMEM((2, 64, D), BF16),
            pltpu.VMEM((64, D), BF16),
            dma((5,)),
            dma((2, 2)),
            dma((7, NX)),
            dma((NX, NQ)),
            dma((2, NX, NQ)),
            dma((3, NX, NQ)),
            dma((4,)),
            dma((2, NX)),
            dma((2, NX)),
            dma((2, NX)),
            dma((4, NX)),
            dma((2, NX, NQ)),
            dma((NQ,)),
            dma((2, NQ)),
            dma((2 * NQ,)),
        ],
        compiler_params=pltpu.CompilerParams(
            collective_id=0, has_side_effects=True, vmem_limit_bytes=63 * 2**20
        ),
        cost_estimate=pl.CostEstimate(
            flops=24_000_000_000, bytes_accessed=24_000_000, transcendentals=4_000_000
        ),
    )(
        tokens, gain_attn.reshape(1, D), w_query, w_key, w_value, w_out, gain_mlp.reshape(1, D),
        jnp.asarray(cos), jnp.asarray(sin),
    )


def solution(mesh):
    placed = (
        P(("dp", "tp"), None),
        P(),
        P(None, "tp"),
        P(None, "tp"),
        P(None, "tp"),
        P("tp", None),
        P(),
    )
    return jax.shard_map(
        sublayer,
        mesh=mesh,
        in_specs=placed,
        out_specs=(P(("dp", "tp"), None), P(("dp", "tp"), None)),
        check_vma=False,
    )
```

time: 586 us -> 152 us (0.26)
  waiting for transfers between devices: 458 us -> 0 us
  Pallas kernels: 0 us -> 138 us
  matrix products: 65.6 us -> 0 us
  other arithmetic: 28.6 us -> 0 us
  between operations: 14.3 us -> 0.64 us
    psum x1 -> x0, waiting for transfers between devices: 363 us -> none  [shards(): lax.psum(jnp.dot(context, w_out, preferred_element_type=jnp.float32).asty...]
    pallas_call x0 -> x1, Pallas kernels: none -> 138 us  [sublayer(): pl.pallas_call(kernel, out_shape=(shape, shape), in_specs=[any_spec, vmem...]
    all_gather x1 -> x0, waiting for transfers between devices: 95 us -> none  [shards(): lax.all_gather(tokens, 'tp', axis=0, tiled=True)]
    dot_general x5 -> x0, matrix products: 55 us -> none  [the longest x1 15.9 us: shards(): jnp.dot(context, w_out, preferred_element_type=jnp.float32)]
    convert_element_type x6 -> x0, other arithmetic: 13.3 us -> none  [the longest x1 9.79 us: shards(): rms_scaled(lax.all_gather(tokens, 'tp', axis=0, tiled=True), gain_attn)]
    sub x1 -> x0, matrix products: 10.6 us -> none  [attend(): soft_weights = jnp.exp(scores - row_top)]
    reduce_sum x2 -> x0, other arithmetic: 7.48 us -> none  [rms_scaled(): jnp.mean(as_float * as_float, axis=-1, keepdims=True) + 1e-05]
  transfers between devices with their start and end apart: 4 -> 0, of which waited for: 2 -> 0; matrix products, arithmetic and copies ran while one was open for 8% -> 0% of each run, Pallas kernels for 0% -> 0%
where the time goes in v1:
time: 152 us; the launch traced here: 151 us
  Pallas kernels  138 us (91%)
  local copies, waits for them, and re-layouts  12.7 us (8%)
    pallas_call x1, Pallas kernels, sublayer(): pl.pallas_call(kernel, out_shape=(shape, shape), in_specs=[any_spec, vmem...  138 us
    unnamed x4, local copies, waits for them, and re-layouts  10 us

profile of v1, /device:TPU:1, one launch (start us, length us, event | category | flops | bytes accessed | tf_op | source)
XLA Modules:
  0.0 151.0 jit_solution(15743611547305073119)
XLA Ops:
  0.6 1.4 reshape.10.gain_attn
  2.0 1.3 reshape.11.gain_mlp
  3.3 2.8 %copy.11.wk_hbm = bf16[8192,64]{1,0:T(8,128)(2,1)} copy(bf16[8192,64]{0,1:T(8,128)(2,1)} %param.12) | data formatting | bytes 2097152 | tf_op args[3]
  6.1 2.7 %copy.12.wv_hbm = bf16[8192,64]{1,0:T(8,128)(2,1)} copy(bf16[8192,64]{0,1:T(8,128)(2,1)} %param.13) | data formatting | bytes 2097152 | tf_op args[4]
  8.8 137.6 %shard_map.104 = (bf16[64,8192]{1,0:T(8,128)(2,1)}, bf16[64,8192]{1,0:T(8,128)(2,1)}) custom-call(bf16[64,8192]{1,0:T(8,128)(2,1)} %tok_hbm.1, bf16[1,8192]{1,0:T(2,128)(2,1)} %reshape.10.gain_attn, bf16[8192,512]{1,0:T(8,128)(2,1)} %wq_hbm.1, bf16[8192,64]{1,0:T(8,128)(2,1)} %copy.11.wk_hbm, bf16[8192,64]{1,0:T(8,128)(2,1)} %copy.12.wv_hbm, ...), custom_call_target="tpu_custom_call" | custom-call | flops 24000000000 | bytes 24000000 | tf_op jit(solution)/shard_map/pallas_call | solution.py:537
  146.4 2.3 %copy.15 = bf16[64,8192]{1,0:T(8,128)(2,1)} copy(bf16[64,8192]{1,0:T(8,128)(2,1)} %get-tuple-element.4) | data formatting | bytes 2097152
  148.7 2.3 %copy.16 = bf16[64,8192]{1,0:T(8,128)(2,1)} copy(bf16[64,8192]{1,0:T(8,128)(2,1)} %get-tuple-element.5) | data formatting | bytes 2097152

commit v2 on v0

v2 whole, which is shorter than its diff:
```python
import math

import jax
import jax.numpy as jnp
import numpy as np
from jax import lax
from jax.experimental import pallas as pl
from jax.experimental.pallas import tpu as pltpu
from jax.sharding import PartitionSpec as P

MESH = pl.DeviceIdType.MESH
BF16 = jnp.bfloat16
F32 = jnp.float32
D = 8192
HD = 128
NX = 4
BLK = 256
PIECE = 2048
NQ = D // PIECE
HEADS = 4
THIRD = D - PIECE


def rotary_tables():
    inverse = np.exp(np.arange(HD // 2) * (-2.0 * math.log(500000.0) / HD))
    angles = np.arange(NX * BLK)[:, None] * inverse[None, :]
    cos = np.repeat(np.cos(angles), 2, axis=1).astype(np.float32)
    sin = np.repeat(np.sin(angles), 2, axis=1)
    sin[:, 0::2] *= -1.0
    return cos, sin.astype(np.float32)


def kernel(
    tok_hbm, gains, wq_hbm, wk_hbm, wv_hbm, wo_hbm, cos_hbm, sin_hbm, out_hbm,
    xs, wq, wkv, wo, qb, kvl, kvr, ctx, ctxr, acc, cos, sin, rz, rz0, rr, rr0, rx, rx0, tok,
    s_in, s_send, s_xr, s_xe, s_zr, s_sib, s_w, s_kvs, s_kvr, s_ctx, s_rsend, s_rz, s_rr, s_rx, s_out,
):
    tp, dp = lax.axis_index("tp"), lax.axis_index("dp")
    x, zl, c = tp // 4, (tp // 2) % 2, tp % 2
    y, zz = dp // 2, (dp % 2) * 2 + zl

    def device(x_to, z_to, c_to):
        return (x_to * 4 + (z_to % 2) * 2 + c_to, y * 2 + z_to // 2)

    right, left = device((x + 1) % 4, zz, c), device((x + 3) % 4, zz, c)
    above, below = device(x, (zz + 1) % 4, c), device(x, (zz + 3) % 4, c)
    across, sibling = device(x, (zz + 2) % 4, c), device(x, zz, 1 - c)
    b_own, b_right, b_far, b_left = x, (x + 1) % 4, (x + 2) % 4, (x + 3) % 4

    def remote(src, dst, send_sem, recv_sem, to):
        return pltpu.make_async_remote_copy(
            src_ref=src, dst_ref=dst, send_sem=send_sem, recv_sem=recv_sem,
            device_id=to, device_id_type=MESH,
        )

    def sent(ref, sem):
        remote(ref, ref, sem, s_w.at[0], sibling).wait_send()

    def landed(ref, sem):
        remote(ref, ref, s_w.at[0], sem, sibling).wait_recv()

    def cols(q):
        return pl.ds(pl.multiple_of(q * PIECE, PIECE), PIECE)

    def rows(start, size):
        return pl.ds(pl.multiple_of(start, 32), size)

    tok_copy = pltpu.make_async_copy(tok_hbm, tok, s_in.at[0])
    tok_copy.start()
    barrier = pltpu.get_barrier_semaphore()
    for neighbour in (right, left, above, below, across, sibling):
        pl.semaphore_signal(barrier, inc=1, device_id=neighbour, device_id_type=MESH)

    wk_rows, wv_rows = rows(c * HD, 64), rows(c * HD + 64, 64)
    in_copies = [
        pltpu.make_async_copy(wk_hbm, wkv.at[wk_rows], s_in.at[1]),
        pltpu.make_async_copy(wv_hbm, wkv.at[wv_rows], s_in.at[2]),
        pltpu.make_async_copy(wq_hbm, wq, s_in.at[3]),
        pltpu.make_async_copy(cos_hbm, cos, s_in.at[4]),
        pltpu.make_async_copy(sin_hbm, sin, s_in.at[5]),
        pltpu.make_async_copy(wo_hbm, wo.at[0], s_in.at[6]),
    ]
    for copy in in_copies:
        copy.start()

    tok_copy.wait()

    def norm_rows(i, carry):
        part = pl.ds(pl.multiple_of(i * 16, 16), 16)
        as_float = tok[part, :].astype(F32)
        inv = lax.rsqrt(jnp.mean(as_float * as_float, axis=-1, keepdims=True) + 1e-05)
        normed = as_float * inv * gains[...].astype(F32)
        xs[x, pl.ds(pl.multiple_of(c * 64 + i * 16, 16), 16), :] = normed.astype(BF16)
        return carry

    lax.fori_loop(0, 4, norm_rows, 0)
    pl.semaphore_wait(barrier, 6)

    from_below = 192 - 64 * zl
    from_above = 128 + 64 * zl
    x_ways = (right, left)

    def part_ref(b, q, kind, core):
        if kind == 0:
            return xs.at[b, rows(core * 64, 64), cols(q)]
        at = (from_below, from_above)[kind - 1]
        return xs.at[b, rows(at + core * 32, 32), cols(q)]

    def half_ref(b, q, way):
        return xs.at[b, rows(c * 64 + 32 * way, 32), cols(q)]

    def send_x(b, q, way):
        ref = part_ref(b, q, 0, c)
        remote(ref, ref, s_send.at[way, b], s_xr.at[way, b, q], x_ways[way]).start()

    def send_half(b, q, way):
        ref = half_ref(b, q, way)
        remote(ref, ref, s_send.at[way, b], s_xr.at[way, b, q], x_ways[way]).start()

    def send_extra(b, kind, way):
        ref = part_ref(b, 0, kind, c)
        remote(ref, ref, s_send.at[7 + way, b], s_xe.at[kind - 1, b], x_ways[way]).start()

    def send_z(b, q):
        for way in range(2):
            at = (from_above, from_below)[way]
            dst = xs.at[b, rows(at + c * 32, 32), cols(q)]
            to = (above, below)[way]
            remote(half_ref(b, q, way), dst, s_send.at[2 + way, b], s_zr.at[way, b, q], to).start()

    def send_sib(b, q, kind):
        ref = part_ref(b, q, kind, c)
        remote(ref, ref, s_send.at[4 + kind, b], s_sib.at[kind, b, q], sibling).start()

    def recv_sib(b, q):
        for kind in range(3):
            landed(part_ref(b, q, kind, 1 - c), s_sib.at[kind, b, q])

    def pass_z(b, q):
        for way in range(2):
            landed(part_ref(b, q, 1 + way, c), s_zr.at[way, b, q])
            send_sib(b, q, 1 + way)

    def start_own(q, carry):
        send_z(b_own, q)

        @pl.when(q > 0)
        def _():
            send_x(b_own, q, 0)
            send_x(b_own, q, 1)

        send_sib(b_own, q, 0)
        return carry

    lax.fori_loop(0, NQ, start_own, 0)
    in_copies[0].wait()
    in_copies[1].wait()
    wkv_sends = [
        remote(wkv.at[wk_rows], wkv.at[wk_rows], s_w.at[0], s_w.at[3], sibling),
        remote(wkv.at[wv_rows], wkv.at[wv_rows], s_w.at[1], s_w.at[4], sibling),
    ]
    wo_send = remote(wo_hbm, wo.at[1], s_w.at[2], s_w.at[5], sibling)
    for copy in wkv_sends:
        copy.start()
    wo_send.start()
    acc[...] = jnp.zeros_like(acc)
    transposed = (((1,), (1,)), ((), ()))

    def qkv(a, b, q):
        held = xs[b, :, cols(q)]
        for n in range(2):
            part = pl.ds(n * 256, 256)
            acc[a, :, part] += jnp.dot(held, wq[cols(q), part], preferred_element_type=F32)
        acc[a, :, pl.ds(512, 256)] += lax.dot_general(
            held, wkv[:, cols(q)], transposed, preferred_element_type=F32
        )

    def table(ref, b):
        at = b * BLK
        far = at + (1 - zl) * 128
        parts = [ref[rows(at + zl * 128, 128), :]]
        for half in (1 - zl, zl):
            for core in range(2):
                parts.append(ref[rows(far + core * 64 + half * 32, 32), :])
        return jnp.concatenate(parts, axis=0)

    def kv_send(b):
        return remote(kvl.at[b, c], kvr.at[b, c], s_kvs.at[0, b], s_kvr.at[0, b], across)

    def kv_pass(b):
        return remote(kvr.at[b, c], kvr.at[b, c], s_kvs.at[1, b], s_kvr.at[1, b], sibling)

    def kv_wait(b):
        landed(kvr.at[b, 1 - c], s_kvr.at[1, b])

    def finish_qkv(a, b):
        cos_rows, sin_rows = table(cos, b), table(sin, b)
        lane = lax.broadcasted_iota(jnp.int32, (BLK, HD), 1)

        def turned(value):
            swapped = jnp.where(lane % 2 == 0, pltpu.roll(value, HD - 1, 1), pltpu.roll(value, 1, 1))
            return value * cos_rows + swapped * sin_rows

        first, second = acc[a, :, 512:640], acc[a, :, 640:768]
        key = turned(jnp.where(lane < 64, first, pltpu.roll(second, 64, 1))).astype(BF16)
        value = jnp.where(lane < 64, pltpu.roll(first, 64, 1), second).T.astype(BF16)
        for half in range(2):
            kvl[b, half, 0:128] = key[half * 128 : half * 128 + 128]
            kvl[b, half, 128:256] = value[:, half * 128 : half * 128 + 128]
        kv_send(b).start()
        scale = HD**-0.5 * math.log2(math.e)
        for h in range(HEADS):
            head = (turned(acc[a, :, h * HD : (h + 1) * HD]) * scale).astype(BF16)
            qb[b, h * 192 : h * 192 + 192] = head[0:192]
            qb[b, 768 + h * 64 : 832 + h * 64] = head[192:256]

    in_copies[2].wait()

    def first_loop(q, carry):
        @pl.when(q > 0)
        def _():
            for b, way in ((b_left, 0), (b_right, 1)):
                landed(part_ref(b, q, 0, c), s_xr.at[way, b, q])
                send_z(b, q)
                send_half(b, q, way)
                send_sib(b, q, 0)

        pass_z(b_own, q)
        recv_sib(b_own, q)

        @pl.when(q == 0)
        def _():
            other = rows((1 - c) * HD, 64), rows((1 - c) * HD + 64, 64)
            landed(wkv.at[other[0]], s_w.at[3])
            landed(wkv.at[other[1]], s_w.at[4])

        qkv(2, b_own, q)
        return carry

    lax.fori_loop(0, NQ, first_loop, 0)
    for way in range(2):
        send_x(b_own, 0, way)
    for way in range(2):
        send_extra(b_own, 1 + way, 0)
        send_extra(b_own, 1 + way, 1)
    in_copies[3].wait()
    in_copies[4].wait()
    finish_qkv(2, b_own)
    acc[2] = jnp.zeros((BLK, 768), F32)

    def both(fn):
        def one(a, carry):
            fn(a, (x + 1 + 2 * a) % 4)
            return carry

        lax.fori_loop(0, 2, one, 0)

    def far_rows(q):
        for way in range(2):
            landed(half_ref(b_far, q, way), s_xr.at[way, b_far, q])

    def second_loop(i, carry):
        q = i + 1
        for b in (b_left, b_right):
            pass_z(b, q)

        def near(a, b):
            recv_sib(b, q)
            qkv(a, b, q)

        both(near)
        far_rows(q)
        send_z(b_far, q)
        send_sib(b_far, q, 0)
        return carry

    lax.fori_loop(0, NQ - 1, second_loop, 0)

    def near_first(kind):
        for b, way in ((b_left, 0), (b_right, 1)):
            landed(part_ref(b, 0, kind, c), s_xr.at[way, b, 0] if kind == 0 else s_xe.at[kind - 1, b])
            if kind == 0:
                send_half(b, 0, way)
            elif kind == way + 1:
                send_extra(b, kind, way)
            send_sib(b, 0, kind)

    def third_loop(i, carry):
        for kind in range(3):
            pl.when(i == kind)(lambda kind=kind: near_first(kind))
        pass_z(b_far, i + 1)
        recv_sib(b_far, i + 1)
        qkv(2, b_far, i + 1)
        return carry

    lax.fori_loop(0, NQ - 1, third_loop, 0)
    kv_send(b_own).wait_recv()
    kv_pass(b_own).start()

    def near_last(a, b):
        recv_sib(b, 0)
        qkv(a, b, 0)
        finish_qkv(a, b)

    both(near_last)
    far_rows(0)
    send_sib(b_far, 0, 0)
    for kind in (1, 2):
        landed(part_ref(b_far, 0, kind, c), s_xe.at[kind - 1, b_far])
        send_sib(b_far, 0, kind)
    recv_sib(b_far, 0)
    qkv(2, b_far, 0)
    finish_qkv(2, b_far)

    for b in (b_right, b_left):
        kv_send(b).wait_recv()
        kv_pass(b).start()
    for b in (b_own, b_right, b_left):
        kv_wait(b)

    def place(row):
        other = row >= 192
        inner = jnp.where(other, row - 192, row - 128)
        half = jnp.where(other, zl, 1 - zl)
        far = (1 - zl) * 128 + (inner // 32) * 64 + half * 32 + inner % 32
        return jnp.where(row < 128, zl * 128 + row, far)

    def attend_step(b, kb, state, masked):
        low = lax.broadcasted_iota(jnp.int32, (HD, HD), 1) < 64

        def joined(mine, theirs):
            key = jnp.concatenate([mine[kb, 0, 0:128], mine[kb, 1, 0:64], theirs[kb, 1, 64:128]], axis=0)
            half = jnp.where(low, mine[kb, 1, 128:256].astype(F32), theirs[kb, 1, 128:256].astype(F32))
            return key, jnp.concatenate([mine[kb, 0, 128:256], half.astype(BF16)], axis=1)

        inside, outside = joined(kvl, kvr), joined(kvr, kvl)
        after = []
        for j in range(4):
            key, value = outside if j == 3 else inside
            top, total, out = state[j]
            at = pl.ds(j * BLK, BLK)
            scores = lax.dot_general(key, qb[b, at], transposed, preferred_element_type=F32)
            if masked:
                column = lax.broadcasted_iota(jnp.int32, (1, BLK), 1)
                column = 192 + column % 64 if j == 3 else (column + j * BLK) % 192
                row = lax.broadcasted_iota(jnp.int32, (BLK, 1), 0)
                scores = jnp.where(place(row) <= place(column), scores, -1e30)
            new_top = jnp.maximum(top, jnp.max(scores, axis=0, keepdims=True))
            weights = jnp.exp2(scores - new_top)
            fade = jnp.exp2(top - new_top)
            total = total * fade + jnp.sum(weights, axis=0, keepdims=True)
            out = out * fade + jnp.dot(value, weights.astype(BF16), preferred_element_type=F32)
            after.append((new_top, total, out))
        return tuple(after)

    def attend(b, before_last=None):
        start = tuple(
            (jnp.full((1, BLK), -1e30, F32), jnp.zeros((1, BLK), F32), jnp.zeros((HD, BLK), F32))
            for _ in range(4)
        )
        state = lax.fori_loop(0, b, lambda kb, s: attend_step(b, kb, s, False), start)
        if before_last is not None:
            before_last()
        state = attend_step(b, b, state, True)
        out = [(value / total).T.astype(BF16) for _, total, value in state]
        inside, outside = jnp.concatenate(out[:3], axis=0), out[3]
        for h in range(HEADS):
            at = pl.ds(h * HD, HD)
            for core in range(2):
                first, second = h * 192 + core * 64, h * 192 + 128 + core * 32
                third = h * 64 + core * 32
                ctx[b, core, 0:64, at] = inside[first : first + 64]
                ctx[b, core, 64:96, at] = inside[second : second + 32]
                ctx[b, core, 96:128, at] = outside[third : third + 32]
        ctx_send(b).start()

    def ctx_send(b):
        return remote(ctx.at[b, 1 - c], ctxr.at[b], s_ctx.at[0, b], s_ctx.at[1, b], sibling)

    def third_cols(q):
        return pl.ds(pl.multiple_of((q - 1) * PIECE, PIECE), PIECE)

    def project(b, q):
        def tile(n, carry):
            at = pl.ds(pl.multiple_of(q * PIECE + n * 512, 512), 512)
            total = jnp.dot(ctx[b, c], wo[0, :, at], preferred_element_type=F32)
            total += jnp.dot(ctxr[b], wo[1, :, at], preferred_element_type=F32)
            xs[b, 0:128, at] = total.astype(BF16)
            return carry

        lax.fori_loop(0, PIECE // 512, tile, 0)

    def rs_z(b, q):
        for way in range(2):
            at = (64 + 32 * zl, 96 - 32 * zl)[way]
            place_in = pl.ds(32 - 32 * way, 32)
            dst = rz0.at[place_in] if isinstance(q, int) else rz.at[b, place_in, third_cols(q)]
            src = xs.at[b, rows(at, 32), cols(q)]
            to = (above, below)[way]
            remote(src, dst, s_rsend.at[way, b], s_rz.at[way, b, q], to).start()

    def drain(b, kind):
        quarter, third = xs.at[b, 0:32], xs.at[b, 0:32, 0:THIRD]
        for way in range(2):
            sent(quarter if kind == "own" else third, s_send.at[2 + way, b])
        for part, ref in enumerate((xs.at[b, 0:64], quarter, quarter)):
            sent(ref, s_send.at[4 + part, b])
        if kind == "own":
            for way in range(2):
                sent(xs.at[b, 0:64], s_send.at[way, b])
                sent(xs.at[b, 0:64, 0:PIECE], s_send.at[7 + way, b])
        elif kind in (0, 1):
            sent(quarter, s_send.at[kind, b])
            sent(xs.at[b, 0:32, 0:PIECE], s_send.at[7 + kind, b])

    def sum_z(b, q):
        for way in range(2):
            landed(rz.at[b, pl.ds(32 - 32 * way, 32), third_cols(q)], s_rz.at[way, b, q])
        return xs[b, 0:64, cols(q)].astype(F32) + rz[b, :, third_cols(q)].astype(F32)

    def relay(q, way):
        part = pl.ds(32 * way, 32)
        to = x_ways[way]
        src, dst = xs.at[b_far, part, cols(q)], rr.at[way, :, cols(q)]
        remote(src, dst, s_rsend.at[2 + way, b_far], s_rr.at[way, q], to).start()
        if isinstance(q, int):
            src = xs.at[b_far, pl.ds(64 + 32 * way, 32), cols(0)]
            remote(src, rr0.at[way], s_rsend.at[4 + way, b_far], s_rr.at[way, NQ], to).start()

    def far_sum(q):
        xs[b_far, 0:64, cols(q)] = sum_z(b_far, q).astype(BF16)
        relay(q, 0)
        relay(q, 1)

    def near_sum_first(way):
        b, to = (b_right, b_left)[way], x_ways[way]
        landed(rr.at[way, :, cols(0)], s_rr.at[way, 0])
        landed(rr0.at[way], s_rr.at[way, NQ])
        for at, term in ((32 * way, rr[way, :, cols(0)]), (64 + 32 * way, rr0[way])):
            total = xs[b, at : at + 32, cols(0)].astype(F32) + term.astype(F32)
            xs[b, at : at + 32, cols(0)] = total.astype(BF16)
        src = xs.at[b, 0:128, cols(0)]
        remote(src, rx0.at[way], s_rsend.at[4 + way, b], s_rx.at[way, 0], to).start()

    def near_sum(q, way):
        b, to = (b_right, b_left)[way], x_ways[way]
        landed(rr.at[way, :, cols(q)], s_rr.at[way, q])
        total = sum_z(b, q)
        term = rr[way, :, cols(q)].astype(F32)
        first, second = total[0:32], total[32:64]
        if way == 0:
            first = first + term
        else:
            second = second + term
        xs[b, 0:32, cols(q)] = first.astype(BF16)
        xs[b, 32:64, cols(q)] = second.astype(BF16)
        dst = rx.at[way, :, third_cols(q)]
        remote(xs.at[b, 0:64, cols(q)], dst, s_rsend.at[2 + way, b], s_rx.at[way, q], to).start()

    def far_kv():
        kv_send(b_far).wait_recv()
        kv_pass(b_far).start()
        kv_wait(b_far)

    attend(b_far, far_kv)
    drain(b_far, "far")
    in_copies[5].wait()
    landed(wo.at[1], s_w.at[5])
    ctx_send(b_far).wait_recv()
    project(b_far, 0)
    relay(0, 0)
    relay(0, 1)

    def far_project(i, carry):
        project(b_far, i + 1)
        rs_z(b_far, i + 1)
        return carry

    lax.fori_loop(0, NQ - 1, far_project, 0)
    drain(b_right, 1)
    drain(b_left, 0)

    def near_project(a, b):
        attend(b)

        def sums(q, carry):
            far_sum(q)
            return carry

        lax.fori_loop(1 + a, 2 + 2 * a, sums, 0)
        ctx_send(b).wait_recv()

        def piece(i, carry):
            q = (i + 1) % NQ
            project(b, q)

            @pl.when(q > 0)
            def _():
                rs_z(b, q)

            return carry

        lax.fori_loop(0, NQ, piece, 0)

    both(near_project)
    near_sum_first(0)
    near_sum_first(1)
    attend(b_own)
    drain(b_own, "own")
    ctx_send(b_own).wait_recv()

    def own_project(i, carry):
        q = (i + 1) % NQ
        project(b_own, q)

        @pl.when(q > 0)
        def _():
            rs_z(b_own, q)

        return carry

    lax.fori_loop(0, NQ, own_project, 0)

    def near_sums(i, carry):
        near_sum(i + 1, 0)
        near_sum(i + 1, 1)
        return carry

    lax.fori_loop(0, NQ - 1, near_sums, 0)

    landed(rx0.at[0], s_rx.at[0, 0])
    landed(rx0.at[1], s_rx.at[1, 0])
    total = xs[b_own, 0:128, cols(0)].astype(F32) + rx0[0].astype(F32) + rx0[1].astype(F32)
    xs[b_own, 0:128, cols(0)] = total.astype(BF16)
    rs_z(b_own, 0)

    def store(q, head_sum):
        tok[:, cols(q)] = (tok[:, cols(q)].astype(F32) + head_sum).astype(BF16)
        pltpu.make_async_copy(tok.at[:, cols(q)], out_hbm.at[:, cols(q)], s_out.at[q]).start()

    def last_sum(q):
        total = sum_z(b_own, q)
        for way in range(2):
            landed(rx.at[way, :, third_cols(q)], s_rx.at[way, q])
        total += rx[0, :, third_cols(q)].astype(F32) + rx[1, :, third_cols(q)].astype(F32)
        store(q, total)

    def last_two(i, carry):
        last_sum(i + 1)
        return carry

    lax.fori_loop(0, 2, last_two, 0)
    for way in range(2):
        landed(rz0.at[pl.ds(32 - 32 * way, 32)], s_rz.at[way, b_own, 0])
    store(0, xs[b_own, 0:64, cols(0)].astype(F32) + rz0[...].astype(F32))
    lax.fori_loop(2, 3, last_two, 0)

    for q in range(NQ):
        pltpu.make_async_copy(tok.at[:, cols(q)], out_hbm.at[:, cols(q)], s_out.at[q]).wait()
    for copy in (*wkv_sends, wo_send):
        copy.wait_send()
    for b in range(NX):
        kv_send(b).wait_send()
        kv_pass(b).wait_send()
        ctx_send(b).wait_send()
    for way in range(2):
        for b in (b_far, b_right, b_left):
            sent(xs.at[b, 0:32, 0:THIRD], s_rsend.at[way, b])
        sent(xs.at[b_own, 0:32], s_rsend.at[way, b_own])
        sent(xs.at[b_far, 0:32], s_rsend.at[2 + way, b_far])
        sent(xs.at[b_far, 0:32, 0:PIECE], s_rsend.at[4 + way, b_far])
        b = (b_right, b_left)[way]
        sent(xs.at[b, 0:64, 0:THIRD], s_rsend.at[2 + way, b])
        sent(xs.at[b, 0:128, 0:PIECE], s_rsend.at[4 + way, b])


def final_norm(stream_in, gain, stream_out, mlp_out):
    stream = stream_in[...]
    stream_out[...] = stream
    as_float = stream.astype(F32)
    inv = lax.rsqrt(jnp.mean(as_float * as_float, axis=-1, keepdims=True) + 1e-05)
    mlp_out[...] = (as_float * inv * gain[...].astype(F32)).astype(BF16)


def sublayer(tokens, gain_attn, w_query, w_key, w_value, w_out, gain_mlp):
    cos, sin = rotary_tables()
    gain_attn, gain_mlp = gain_attn.reshape(1, D), gain_mlp.reshape(1, D)
    any_spec = pl.BlockSpec(memory_space=pl.ANY)
    vmem_spec = pl.BlockSpec(memory_space=pltpu.VMEM)
    dma = pltpu.SemaphoreType.DMA
    shape = jax.ShapeDtypeStruct((64, D), BF16)
    stream = pl.pallas_call(
        kernel,
        out_shape=shape,
        in_specs=[any_spec, vmem_spec] + [any_spec] * 6,
        out_specs=any_spec,
        scratch_shapes=[
            pltpu.VMEM((NX, BLK, D), BF16),
            pltpu.VMEM((D, 512), BF16),
            pltpu.VMEM((256, D), BF16),
            pltpu.VMEM((2, 512, D), BF16),
            pltpu.VMEM((NX, HEADS * BLK, HD), BF16),
            pltpu.VMEM((NX, 2, 256, HD), BF16),
            pltpu.VMEM((NX, 2, 256, HD), BF16),
            pltpu.VMEM((NX, 2, 128, 512), BF16),
            pltpu.VMEM((NX, 128, 512), BF16),
            pltpu.VMEM((3, BLK, 768), F32),
            pltpu.VMEM((NX * BLK, HD), F32),
            pltpu.VMEM((NX * BLK, HD), F32),
            pltpu.VMEM((NX, 64, THIRD), BF16),
            pltpu.VMEM((64, PIECE), BF16),
            pltpu.VMEM((2, 32, D), BF16),
            pltpu.VMEM((2, 32, PIECE), BF16),
            pltpu.VMEM((2, 64, THIRD), BF16),
            pltpu.VMEM((2, 128, PIECE), BF16),
            pltpu.VMEM((64, D), BF16),
            dma((7,)),
            dma((9, NX)),
            dma((2, NX, NQ)),
            dma((2, NX)),
            dma((2, NX, NQ)),
            dma((3, NX, NQ)),
            dma((6,)),
            dma((2, NX)),
            dma((2, NX)),
            dma((2, NX)),
            dma((6, NX)),
            dma((2, NX, NQ)),
            dma((2, NQ + 1)),
            dma((2, NQ)),
            dma((NQ,)),
        ],
        compiler_params=pltpu.CompilerParams(
            collective_id=0, has_side_effects=True, vmem_limit_bytes=63 * 2**20
        ),
        cost_estimate=pl.CostEstimate(
            flops=24_000_000_000, bytes_accessed=24_000_000, transcendentals=4_000_000
        ),
    )(
        tokens, gain_attn, w_query, w_key.T, w_value.T, w_out, jnp.asarray(cos), jnp.asarray(sin),
    )
    block = pl.BlockSpec((16, D), lambda i: (i, 0))
    return pl.pallas_call(
        final_norm,
        grid=(4,),
        out_shape=(shape, shape),
        in_specs=[block, pl.BlockSpec((1, D), lambda i: (0, 0))],
        out_specs=(block, block),
        compiler_params=pltpu.CompilerParams(vmem_limit_bytes=8 * 2**20),
        cost_estimate=pl.CostEstimate(flops=3_000_000, bytes_accessed=3_000_000, transcendentals=64),
    )(stream, gain_mlp)


def solution(mesh):
    placed = (
        P(("dp", "tp"), None),
        P(),
        P(None, "tp"),
        P(None, "tp"),
        P(None, "tp"),
        P("tp", None),
        P(),
    )
    return jax.shard_map(
        sublayer,
        mesh=mesh,
        in_specs=placed,
        out_specs=(P(("dp", "tp"), None), P(("dp", "tp"), None)),
        check_vma=False,
    )
```

time: 586 us -> 133 us (0.23)
  waiting for transfers between devices: 458 us -> 0 us
  Pallas kernels: 0 us -> 128 us
  matrix products: 65.6 us -> 0 us
  other arithmetic: 28.6 us -> 0 us
  local copies, waits for them, and re-layouts: 18.1 us -> 3.3 us
  between operations: 14.3 us -> 0.65 us
    psum x1 -> x0, waiting for transfers between devices: 363 us -> none  [shards(): lax.psum(jnp.dot(context, w_out, preferred_element_type=jnp.float32).asty...]
    pallas_call x0 -> x2, Pallas kernels: none -> 128 us  [the longest x1 126 us: sublayer(): pl.pallas_call(kernel, out_shape=shape, in_specs=[any_spec, vmem_spec] +...]
    all_gather x1 -> x0, waiting for transfers between devices: 95 us -> none  [shards(): lax.all_gather(tokens, 'tp', axis=0, tiled=True)]
    dot_general x5 -> x0, matrix products: 55 us -> none  [the longest x1 15.9 us: shards(): jnp.dot(context, w_out, preferred_element_type=jnp.float32)]
    convert_element_type x6 -> x0, other arithmetic: 13.3 us -> none  [the longest x1 9.79 us: shards(): rms_scaled(lax.all_gather(tokens, 'tp', axis=0, tiled=True), gain_attn)]
    sub x1 -> x0, matrix products: 10.6 us -> none  [attend(): soft_weights = jnp.exp(scores - row_top)]
    unnamed x16 -> x2, local copies, waits for them, and re-layouts: 10.5 us -> 1.22 us
    reduce_sum x2 -> x0, other arithmetic: 7.48 us -> none  [rms_scaled(): jnp.mean(as_float * as_float, axis=-1, keepdims=True) + 1e-05]
  transfers between devices with their start and end apart: 4 -> 0, of which waited for: 2 -> 0; matrix products, arithmetic and copies ran while one was open for 8% -> 0% of each run, Pallas kernels for 0% -> 0%
where the time goes in v2:
time: 133 us; the launch traced here: 132 us
  Pallas kernels  128 us (96%)
  local copies, waits for them, and re-layouts  3.3 us (2%)
    pallas_call x1, Pallas kernels, sublayer(): pl.pallas_call(kernel, out_shape=shape, in_specs=[any_spec, vmem_spec] +...  126 us

profile of v2, /device:TPU:1, one launch (start us, length us, event | category | flops | bytes accessed | tf_op | source)
XLA Modules:
  0.0 132.2 jit_solution(13785211231238031068)
XLA Ops:
  0.6 1.4 %reshape.10.gains = bf16[1,8192]{1,0:T(2,128)(2,1)} reshape(bf16[8192]{0:T(1024)(128)(2,1)} %param.10) | data formatting | bytes 32768 | tf_op jit(solution)/shard_map/reshape | solution.py:587
  2.0 0.7 reshape.11.gain
  2.7 126.1 %shard_map.104.stream_in = bf16[64,8192]{1,0:T(8,128)(2,1)} custom-call(bf16[64,8192]{1,0:T(8,128)(2,1)} %tok_hbm.1, bf16[1,8192]{1,0:T(2,128)(2,1)} %reshape.10.gains, bf16[8192,512]{1,0:T(8,128)(2,1)} %wq_hbm.1, bf16[64,8192]{1,0:T(8,128)(2,1)} %bitcast.2, bf16[64,8192]{1,0:T(8,128)(2,1)} %bitcast.3, bf16[512,8192]{1,0:T(8,128)(2,1)} %wo_hbm.1, ...), custom_call_target="tpu_custom_call" | custom-call | flops 24000000000 | bytes 24000000 | tf_op jit(solution)/shard_map/pallas_call | solution.py:592
  128.9 0.0 copy-start
  128.9 1.2 copy-done
  130.1 2.1 %shard_map.105 = (bf16[64,8192]{1,0:T(8,128)(2,1)}, bf16[64,8192]{1,0:T(8,128)(2,1)}) custom-call(bf16[64,8192]{1,0:T(8,128)(2,1)S(1)} %copy-done, bf16[1,8192]{1,0:T(2,128)(2,1)S(1)} %reshape.11.gain), custom_call_target="tpu_custom_call" | custom-call | flops 3000000 | bytes 3000000 | tf_op jit(solution)/shard_map/pallas_call | solution.py:643
Async XLA Ops:
  128.9 1.2 copy-start

commit v3 on v2

--- a/solution.py
+++ b/solution.py
@@ -19,6 +19,11 @@
 NQ = D // PIECE
 HEADS = 4
 THIRD = D - PIECE
+FIRST = 1280
+REST = (D - FIRST) // 3
+WO_PARTS = 8
+NCH = 8
+CHUNK = HEADS * BLK // NCH
 
 
 def rotary_tables():
@@ -159,21 +164,30 @@
         remote(wkv.at[wk_rows], wkv.at[wk_rows], s_w.at[0], s_w.at[3], sibling),
         remote(wkv.at[wv_rows], wkv.at[wv_rows], s_w.at[1], s_w.at[4], sibling),
     ]
-    wo_send = remote(wo_hbm, wo.at[1], s_w.at[2], s_w.at[5], sibling)
     for copy in wkv_sends:
         copy.start()
-    wo_send.start()
+
+    def wo_part(k):
+        part = rows(k * (512 // WO_PARTS), 512 // WO_PARTS)
+        return remote(wo_hbm.at[part], wo.at[1, part], s_w.at[2], s_w.at[5], sibling)
+
     acc[...] = jnp.zeros_like(acc)
     transposed = (((1,), (1,)), ((), ()))
 
-    def qkv(a, b, q):
+    def qkv_q(a, b, q):
         held = xs[b, :, cols(q)]
         for n in range(2):
             part = pl.ds(n * 256, 256)
             acc[a, :, part] += jnp.dot(held, wq[cols(q), part], preferred_element_type=F32)
+
+    def qkv_kv(a, b, q):
         acc[a, :, pl.ds(512, 256)] += lax.dot_general(
-            held, wkv[:, cols(q)], transposed, preferred_element_type=F32
+            xs[b, :, cols(q)], wkv[:, cols(q)], transposed, preferred_element_type=F32
         )
+
+    def qkv(a, b, q):
+        qkv_q(a, b, q)
+        qkv_kv(a, b, q)
 
     def table(ref, b):
         at = b * BLK
@@ -193,26 +207,31 @@
     def kv_wait(b):
         landed(kvr.at[b, 1 - c], s_kvr.at[1, b])
 
-    def finish_qkv(a, b):
-        cos_rows, sin_rows = table(cos, b), table(sin, b)
+    def turned(value, b):
         lane = lax.broadcasted_iota(jnp.int32, (BLK, HD), 1)
-
-        def turned(value):
-            swapped = jnp.where(lane % 2 == 0, pltpu.roll(value, HD - 1, 1), pltpu.roll(value, 1, 1))
-            return value * cos_rows + swapped * sin_rows
-
+        swapped = jnp.where(lane % 2 == 0, pltpu.roll(value, HD - 1, 1), pltpu.roll(value, 1, 1))
+        return value * table(cos, b) + swapped * table(sin, b)
+
+    def finish_kv(a, b):
+        lane = lax.broadcasted_iota(jnp.int32, (BLK, HD), 1)
         first, second = acc[a, :, 512:640], acc[a, :, 640:768]
-        key = turned(jnp.where(lane < 64, first, pltpu.roll(second, 64, 1))).astype(BF16)
+        key = turned(jnp.where(lane < 64, first, pltpu.roll(second, 64, 1)), b).astype(BF16)
         value = jnp.where(lane < 64, pltpu.roll(first, 64, 1), second).T.astype(BF16)
         for half in range(2):
             kvl[b, half, 0:128] = key[half * 128 : half * 128 + 128]
             kvl[b, half, 128:256] = value[:, half * 128 : half * 128 + 128]
         kv_send(b).start()
+
+    def finish_q(a, b):
         scale = HD**-0.5 * math.log2(math.e)
         for h in range(HEADS):
-            head = (turned(acc[a, :, h * HD : (h + 1) * HD]) * scale).astype(BF16)
+            head = (turned(acc[a, :, h * HD : (h + 1) * HD], b) * scale).astype(BF16)
             qb[b, h * 192 : h * 192 + 192] = head[0:192]
             qb[b, 768 + h * 64 : 832 + h * 64] = head[192:256]
+
+    def finish_qkv(a, b):
+        finish_kv(a, b)
+        finish_q(a, b)
 
     in_copies[2].wait()
 
@@ -226,6 +245,7 @@
                 send_sib(b, q, 0)
 
         pass_z(b_own, q)
+        wo_part(q).start()
         recv_sib(b_own, q)
 
         @pl.when(q == 0)
@@ -240,9 +260,9 @@
     lax.fori_loop(0, NQ, first_loop, 0)
     for way in range(2):
         send_x(b_own, 0, way)
-    for way in range(2):
-        send_extra(b_own, 1 + way, 0)
-        send_extra(b_own, 1 + way, 1)
+    for turn in range(2):
+        for way in range(2):
+            send_extra(b_own, 1 + (way + turn) % 2, way)
     in_copies[3].wait()
     in_copies[4].wait()
     finish_qkv(2, b_own)
@@ -272,18 +292,23 @@
         far_rows(q)
         send_z(b_far, q)
         send_sib(b_far, q, 0)
+        wo_part(4 + i).start()
         return carry
 
     lax.fori_loop(0, NQ - 1, second_loop, 0)
 
-    def near_first(kind):
+    def near_first(turn):
         for b, way in ((b_left, 0), (b_right, 1)):
-            landed(part_ref(b, 0, kind, c), s_xr.at[way, b, 0] if kind == 0 else s_xe.at[kind - 1, b])
-            if kind == 0:
+            if turn == 0:
+                landed(part_ref(b, 0, 0, c), s_xr.at[way, b, 0])
                 send_half(b, 0, way)
-            elif kind == way + 1:
-                send_extra(b, kind, way)
-            send_sib(b, 0, kind)
+                send_sib(b, 0, 0)
+            else:
+                kind = 1 + (way + turn - 1) % 2
+                landed(part_ref(b, 0, kind, c), s_xe.at[kind - 1, b])
+                if turn == 1:
+                    send_extra(b, kind, way)
+                send_sib(b, 0, kind)
 
     def third_loop(i, carry):
         for kind in range(3):
@@ -303,14 +328,17 @@
         finish_qkv(a, b)
 
     both(near_last)
+    wo_part(7).start()
     far_rows(0)
     send_sib(b_far, 0, 0)
     for kind in (1, 2):
         landed(part_ref(b_far, 0, kind, c), s_xe.at[kind - 1, b_far])
         send_sib(b_far, 0, kind)
     recv_sib(b_far, 0)
-    qkv(2, b_far, 0)
-    finish_qkv(2, b_far)
+    qkv_kv(2, b_far, 0)
+    finish_kv(2, b_far)
+    qkv_q(2, b_far, 0)
+    finish_q(2, b_far)
 
     for b in (b_right, b_left):
         kv_send(b).wait_recv()
@@ -335,35 +363,44 @@
 
         inside, outside = joined(kvl, kvr), joined(kvr, kvl)
         after = []
-        for j in range(4):
-            key, value = outside if j == 3 else inside
-            top, total, out = state[j]
-            at = pl.ds(j * BLK, BLK)
-            scores = lax.dot_general(key, qb[b, at], transposed, preferred_element_type=F32)
+        for group in range(0, NCH, NCH // 2):
+            part = range(group, group + NCH // 2)
+            sides = {j: inside if j * CHUNK < 768 else outside for j in part}
+            scores = {
+                j: lax.dot_general(
+                    sides[j][0], qb[b, pl.ds(j * CHUNK, CHUNK)], transposed, preferred_element_type=F32
+                )
+                for j in part
+            }
             if masked:
-                column = lax.broadcasted_iota(jnp.int32, (1, BLK), 1)
-                column = 192 + column % 64 if j == 3 else (column + j * BLK) % 192
-                row = lax.broadcasted_iota(jnp.int32, (BLK, 1), 0)
-                scores = jnp.where(place(row) <= place(column), scores, -1e30)
-            new_top = jnp.maximum(top, jnp.max(scores, axis=0, keepdims=True))
-            weights = jnp.exp2(scores - new_top)
-            fade = jnp.exp2(top - new_top)
-            total = total * fade + jnp.sum(weights, axis=0, keepdims=True)
-            out = out * fade + jnp.dot(value, weights.astype(BF16), preferred_element_type=F32)
-            after.append((new_top, total, out))
+                column = lax.broadcasted_iota(jnp.int32, (1, CHUNK), 1)
+                row = place(lax.broadcasted_iota(jnp.int32, (BLK, 1), 0))
+                for j in part:
+                    at = j * CHUNK
+                    query = (column + at) % 192 if at < 768 else 192 + (column + at - 768) % 64
+                    scores[j] = jnp.where(row <= place(query), scores[j], -1e30)
+            tops = {
+                j: jnp.maximum(state[j][0], jnp.max(scores[j], axis=0, keepdims=True)) for j in part
+            }
+            weights = {j: jnp.exp2(scores[j] - tops[j]) for j in part}
+            for j in part:
+                fade = jnp.exp2(state[j][0] - tops[j])
+                whole = state[j][1] * fade + jnp.sum(weights[j], axis=0, keepdims=True)
+                term = jnp.dot(sides[j][1], weights[j].astype(BF16), preferred_element_type=F32)
+                after.append((tops[j], whole, state[j][2] * fade + term))
         return tuple(after)
 
     def attend(b, before_last=None):
         start = tuple(
-            (jnp.full((1, BLK), -1e30, F32), jnp.zeros((1, BLK), F32), jnp.zeros((HD, BLK), F32))
-            for _ in range(4)
+            (jnp.full((1, CHUNK), -1e30, F32), jnp.zeros((1, CHUNK), F32), jnp.zeros((HD, CHUNK), F32))
+            for _ in range(NCH)
         )
         state = lax.fori_loop(0, b, lambda kb, s: attend_step(b, kb, s, False), start)
         if before_last is not None:
             before_last()
         state = attend_step(b, b, state, True)
-        out = [(value / total).T.astype(BF16) for _, total, value in state]
-        inside, outside = jnp.concatenate(out[:3], axis=0), out[3]
+        out = [(value / whole).T.astype(BF16) for _, whole, value in state]
+        inside, outside = jnp.concatenate(out[:6], axis=0), jnp.concatenate(out[6:], axis=0)
         for h in range(HEADS):
             at = pl.ds(h * HD, HD)
             for core in range(2):
@@ -377,25 +414,31 @@
     def ctx_send(b):
         return remote(ctx.at[b, 1 - c], ctxr.at[b], s_ctx.at[0, b], s_ctx.at[1, b], sibling)
 
+    def far_kv():
+        kv_send(b_far).wait_recv()
+        kv_pass(b_far).start()
+        kv_wait(b_far)
+
     def third_cols(q):
-        return pl.ds(pl.multiple_of((q - 1) * PIECE, PIECE), PIECE)
+        return pl.ds(pl.multiple_of((q - 1) * REST, REST), REST)
+
+    def sum_cols(q):
+        if isinstance(q, int) and q == 0:
+            return pl.ds(0, FIRST)
+        return pl.ds(pl.multiple_of(FIRST + (q - 1) * REST, 256), REST)
 
     def project(b, q):
-        def tile(n, carry):
-            at = pl.ds(pl.multiple_of(q * PIECE + n * 512, 512), 512)
-            total = jnp.dot(ctx[b, c], wo[0, :, at], preferred_element_type=F32)
-            total += jnp.dot(ctxr[b], wo[1, :, at], preferred_element_type=F32)
-            xs[b, 0:128, at] = total.astype(BF16)
-            return carry
-
-        lax.fori_loop(0, PIECE // 512, tile, 0)
+        at = sum_cols(q)
+        term = jnp.dot(ctx[b, c], wo[0, :, at], preferred_element_type=F32)
+        term += jnp.dot(ctxr[b], wo[1, :, at], preferred_element_type=F32)
+        xs[b, 0:128, at] = term.astype(BF16)
 
     def rs_z(b, q):
         for way in range(2):
             at = (64 + 32 * zl, 96 - 32 * zl)[way]
             place_in = pl.ds(32 - 32 * way, 32)
             dst = rz0.at[place_in] if isinstance(q, int) else rz.at[b, place_in, third_cols(q)]
-            src = xs.at[b, rows(at, 32), cols(q)]
+            src = xs.at[b, rows(at, 32), sum_cols(q)]
             to = (above, below)[way]
             remote(src, dst, s_rsend.at[way, b], s_rz.at[way, b, q], to).start()
 
@@ -416,51 +459,46 @@
     def sum_z(b, q):
         for way in range(2):
             landed(rz.at[b, pl.ds(32 - 32 * way, 32), third_cols(q)], s_rz.at[way, b, q])
-        return xs[b, 0:64, cols(q)].astype(F32) + rz[b, :, third_cols(q)].astype(F32)
+        return xs[b, 0:64, sum_cols(q)].astype(F32) + rz[b, :, third_cols(q)].astype(F32)
 
     def relay(q, way):
         part = pl.ds(32 * way, 32)
         to = x_ways[way]
-        src, dst = xs.at[b_far, part, cols(q)], rr.at[way, :, cols(q)]
+        src, dst = xs.at[b_far, part, sum_cols(q)], rr.at[way, :, sum_cols(q)]
         remote(src, dst, s_rsend.at[2 + way, b_far], s_rr.at[way, q], to).start()
         if isinstance(q, int):
-            src = xs.at[b_far, pl.ds(64 + 32 * way, 32), cols(0)]
+            src = xs.at[b_far, pl.ds(64 + 32 * way, 32), sum_cols(0)]
             remote(src, rr0.at[way], s_rsend.at[4 + way, b_far], s_rr.at[way, NQ], to).start()
 
     def far_sum(q):
-        xs[b_far, 0:64, cols(q)] = sum_z(b_far, q).astype(BF16)
+        xs[b_far, 0:64, sum_cols(q)] = sum_z(b_far, q).astype(BF16)
         relay(q, 0)
         relay(q, 1)
 
     def near_sum_first(way):
         b, to = (b_right, b_left)[way], x_ways[way]
-        landed(rr.at[way, :, cols(0)], s_rr.at[way, 0])
+        landed(rr.at[way, :, sum_cols(0)], s_rr.at[way, 0])
         landed(rr0.at[way], s_rr.at[way, NQ])
-        for at, term in ((32 * way, rr[way, :, cols(0)]), (64 + 32 * way, rr0[way])):
-            total = xs[b, at : at + 32, cols(0)].astype(F32) + term.astype(F32)
-            xs[b, at : at + 32, cols(0)] = total.astype(BF16)
-        src = xs.at[b, 0:128, cols(0)]
+        for at, term in ((32 * way, rr[way, :, sum_cols(0)]), (64 + 32 * way, rr0[way])):
+            total = xs[b, at : at + 32, sum_cols(0)].astype(F32) + term.astype(F32)
+            xs[b, at : at + 32, sum_cols(0)] = total.astype(BF16)
+        src = xs.at[b, 0:128, sum_cols(0)]
         remote(src, rx0.at[way], s_rsend.at[4 + way, b], s_rx.at[way, 0], to).start()
 
     def near_sum(q, way):
         b, to = (b_right, b_left)[way], x_ways[way]
-        landed(rr.at[way, :, cols(q)], s_rr.at[way, q])
+        landed(rr.at[way, :, sum_cols(q)], s_rr.at[way, q])
         total = sum_z(b, q)
-        term = rr[way, :, cols(q)].astype(F32)
+        term = rr[way, :, sum_cols(q)].astype(F32)
         first, second = total[0:32], total[32:64]
         if way == 0:
             first = first + term
         else:
             second = second + term
-        xs[b, 0:32, cols(q)] = first.astype(BF16)
-        xs[b, 32:64, cols(q)] = second.astype(BF16)
+        xs[b, 0:32, sum_cols(q)] = first.astype(BF16)
+        xs[b, 32:64, sum_cols(q)] = second.astype(BF16)
         dst = rx.at[way, :, third_cols(q)]
-        remote(xs.at[b, 0:64, cols(q)], dst, s_rsend.at[2 + way, b], s_rx.at[way, q], to).start()
-
-    def far_kv():
-        kv_send(b_far).wait_recv()
-        kv_pass(b_far).start()
-        kv_wait(b_far)
+        remote(xs.at[b, 0:64, sum_cols(q)], dst, s_rsend.at[2 + way, b], s_rx.at[way, q], to).start()
 
     attend(b_far, far_kv)
     drain(b_far, "far")
@@ -490,53 +528,42 @@
         lax.fori_loop(1 + a, 2 + 2 * a, sums, 0)
         ctx_send(b).wait_recv()
 
-        def piece(i, carry):
-            q = (i + 1) % NQ
+        def piece(q, carry):
             project(b, q)
-
-            @pl.when(q > 0)
-            def _():
-                rs_z(b, q)
-
+            rs_z(b, q)
             return carry
 
-        lax.fori_loop(0, NQ, piece, 0)
+        lax.fori_loop(1, 2, piece, 0)
+        project(b, 0)
+        for way in range(2):
+            pl.when(a == way)(lambda way=way: near_sum_first(way))
+        lax.fori_loop(2, NQ, piece, 0)
 
     both(near_project)
-    near_sum_first(0)
-    near_sum_first(1)
     attend(b_own)
     drain(b_own, "own")
     ctx_send(b_own).wait_recv()
 
-    def own_project(i, carry):
-        q = (i + 1) % NQ
+    def own_project(q, carry):
         project(b_own, q)
-
-        @pl.when(q > 0)
-        def _():
-            rs_z(b_own, q)
-
-        return carry
-
-    lax.fori_loop(0, NQ, own_project, 0)
-
-    def near_sums(i, carry):
-        near_sum(i + 1, 0)
-        near_sum(i + 1, 1)
-        return carry
-
-    lax.fori_loop(0, NQ - 1, near_sums, 0)
+        rs_z(b_own, q)
+        near_sum(q, 0)
+        near_sum(q, 1)
+        return carry
+
+    lax.fori_loop(1, NQ, own_project, 0)
+    project(b_own, 0)
 
     landed(rx0.at[0], s_rx.at[0, 0])
     landed(rx0.at[1], s_rx.at[1, 0])
-    total = xs[b_own, 0:128, cols(0)].astype(F32) + rx0[0].astype(F32) + rx0[1].astype(F32)
-    xs[b_own, 0:128, cols(0)] = total.astype(BF16)
+    whole = xs[b_own, 0:128, sum_cols(0)].astype(F32) + rx0[0].astype(F32) + rx0[1].astype(F32)
+    xs[b_own, 0:128, sum_cols(0)] = whole.astype(BF16)
     rs_z(b_own, 0)
 
     def store(q, head_sum):
-        tok[:, cols(q)] = (tok[:, cols(q)].astype(F32) + head_sum).astype(BF16)
-        pltpu.make_async_copy(tok.at[:, cols(q)], out_hbm.at[:, cols(q)], s_out.at[q]).start()
+        at = sum_cols(q)
+        tok[:, at] = (tok[:, at].astype(F32) + head_sum).astype(BF16)
+        pltpu.make_async_copy(tok.at[:, at], out_hbm.at[:, at], s_out.at[q]).start()
 
     def last_sum(q):
         total = sum_z(b_own, q)
@@ -552,26 +579,27 @@
     lax.fori_loop(0, 2, last_two, 0)
     for way in range(2):
         landed(rz0.at[pl.ds(32 - 32 * way, 32)], s_rz.at[way, b_own, 0])
-    store(0, xs[b_own, 0:64, cols(0)].astype(F32) + rz0[...].astype(F32))
+    store(0, xs[b_own, 0:64, sum_cols(0)].astype(F32) + rz0[...].astype(F32))
     lax.fori_loop(2, 3, last_two, 0)
 
     for q in range(NQ):
-        pltpu.make_async_copy(tok.at[:, cols(q)], out_hbm.at[:, cols(q)], s_out.at[q]).wait()
-    for copy in (*wkv_sends, wo_send):
+        pltpu.make_async_copy(tok.at[:, sum_cols(q)], out_hbm.at[:, sum_cols(q)], s_out.at[q]).wait()
+    for copy in wkv_sends:
         copy.wait_send()
+    sent(wo.at[1], s_w.at[2])
     for b in range(NX):
         kv_send(b).wait_send()
         kv_pass(b).wait_send()
         ctx_send(b).wait_send()
     for way in range(2):
         for b in (b_far, b_right, b_left):
-            sent(xs.at[b, 0:32, 0:THIRD], s_rsend.at[way, b])
+            sent(xs.at[b, 0:32, 0 : 3 * REST], s_rsend.at[way, b])
         sent(xs.at[b_own, 0:32], s_rsend.at[way, b_own])
         sent(xs.at[b_far, 0:32], s_rsend.at[2 + way, b_far])
-        sent(xs.at[b_far, 0:32, 0:PIECE], s_rsend.at[4 + way, b_far])
+        sent(xs.at[b_far, 0:32, 0:FIRST], s_rsend.at[4 + way, b_far])
         b = (b_right, b_left)[way]
-        sent(xs.at[b, 0:64, 0:THIRD], s_rsend.at[2 + way, b])
-        sent(xs.at[b, 0:128, 0:PIECE], s_rsend.at[4 + way, b])
+        sent(xs.at[b, 0:64, 0 : 3 * REST], s_rsend.at[2 + way, b])
+        sent(xs.at[b, 0:128, 0:FIRST], s_rsend.at[4 + way, b])
 
 
 def final_norm(stream_in, gain, stream_out, mlp_out):
@@ -607,12 +635,12 @@
             pltpu.VMEM((3, BLK, 768), F32),
             pltpu.VMEM((NX * BLK, HD), F32),
             pltpu.VMEM((NX * BLK, HD), F32),
-            pltpu.VMEM((NX, 64, THIRD), BF16),
-            pltpu.VMEM((64, PIECE), BF16),
+            pltpu.VMEM((NX, 64, 3 * REST), BF16),
+            pltpu.VMEM((64, FIRST), BF16),
             pltpu.VMEM((2, 32, D), BF16),
-            pltpu.VMEM((2, 32, PIECE), BF16),
-            pltpu.VMEM((2, 64, THIRD), BF16),
-            pltpu.VMEM((2, 128, PIECE), BF16),
+            pltpu.VMEM((2, 32, FIRST), BF16),
+            pltpu.VMEM((2, 64, 3 * REST), BF16),
+            pltpu.VMEM((2, 128, FIRST), BF16),
             pltpu.VMEM((64, D), BF16),
             dma((7,)),
             dma((9, NX)),
@@ -646,7 +674,7 @@
         out_shape=(shape, shape),
         in_specs=[block, pl.BlockSpec((1, D), lambda i: (0, 0))],
         out_specs=(block, block),
-        compiler_params=pltpu.CompilerParams(vmem_limit_bytes=8 * 2**20),
+        compiler_params=pltpu.CompilerParams(vmem_limit_bytes=60 * 2**20),
         cost_estimate=pl.CostEstimate(flops=3_000_000, bytes_accessed=3_000_000, transcendentals=64),
     )(stream, gain_mlp)
 

time: 133 us -> 128 us (0.962)
  Pallas kernels: 128 us -> 123 us
    pallas_call x1, Pallas kernels: 126 us -> 119 us  [sublayer(): pl.pallas_call(kernel, out_shape=shape, in_specs=[any_spec, vmem_spec] +...]
    pallas_call x1, Pallas kernels: 2.13 us -> 3.81 us  [sublayer(): pl.pallas_call(final_norm, grid=(4,), out_shape=(shape, shape), in_specs=...]
where the time goes in v3:
time: 128 us; the launch traced here: 126 us
  Pallas kernels  123 us (96%)
  local copies, waits for them, and re-layouts  2.68 us (2%)
    pallas_call x1, Pallas kernels, sublayer(): pl.pallas_call(kernel, out_shape=shape, in_specs=[any_spec, vmem_spec] +...  119 us
    pallas_call x1, Pallas kernels, sublayer(): pl.pallas_call(final_norm, grid=(4,), out_shape=(shape, shape), in_specs=...  3.81 us
    reshape x2, local copies, waits for them, and re-layouts, sublayer(): gain_attn, gain_mlp = (gain_attn.reshape(1, D), gain_mlp.reshape(1, D))  2.68 us

profile of v3, /device:TPU:1, one launch (start us, length us, event | category | flops | bytes accessed | tf_op | source)
XLA Modules:
  0.0 126.4 jit_solution(7928119962074789254)
XLA Ops:
  0.6 1.4 %reshape.10.gains = bf16[1,8192]{1,0:T(2,128)(2,1)} reshape(bf16[8192]{0:T(1024)(128)(2,1)} %param.10) | data formatting | bytes 32768 | tf_op jit(solution)/shard_map/reshape | solution.py:615
  2.0 1.3 %reshape.11.gain = bf16[1,8192]{1,0:T(2,128)(2,1)} reshape(bf16[8192]{0:T(1024)(128)(2,1)} %param.15) | data formatting | bytes 32768 | tf_op jit(solution)/shard_map/reshape | solution.py:615
  3.3 119.2 %shard_map.104.stream_in = bf16[64,8192]{1,0:T(8,128)(2,1)} custom-call(bf16[64,8192]{1,0:T(8,128)(2,1)} %tok_hbm.1, bf16[1,8192]{1,0:T(2,128)(2,1)} %reshape.10.gains, bf16[8192,512]{1,0:T(8,128)(2,1)} %wq_hbm.1, bf16[64,8192]{1,0:T(8,128)(2,1)} %bitcast.2, bf16[64,8192]{1,0:T(8,128)(2,1)} %bitcast.3, bf16[512,8192]{1,0:T(8,128)(2,1)} %wo_hbm.1, ...), custom_call_target="tpu_custom_call" | custom-call | flops 24000000000 | bytes 24000000 | tf_op jit(solution)/shard_map/pallas_call | solution.py:620
  122.6 3.8 %shard_map.105 = (bf16[64,8192]{1,0:T(8,128)(2,1)}, bf16[64,8192]{1,0:T(8,128)(2,1)}) custom-call(bf16[64,8192]{1,0:T(8,128)(2,1)} %shard_map.104.stream_in, bf16[1,8192]{1,0:T(2,128)(2,1)} %reshape.11.gain), custom_call_target="tpu_custom_call" | custom-call | flops 3000000 | bytes 3000000 | tf_op jit(solution)/shard_map/pallas_call | solution.py:671

commit v4 on v3

--- a/solution.py
+++ b/solution.py
@@ -22,6 +22,7 @@
 FIRST = 1280
 REST = (D - FIRST) // 3
 WO_PARTS = 8
+REST_OF_ROW = (1, 2, 3)
 NCH = 8
 CHUNK = HEADS * BLK // NCH
 
@@ -38,7 +39,7 @@
 def kernel(
     tok_hbm, gains, wq_hbm, wk_hbm, wv_hbm, wo_hbm, cos_hbm, sin_hbm, out_hbm,
     xs, wq, wkv, wo, qb, kvl, kvr, ctx, ctxr, acc, cos, sin, rz, rz0, rr, rr0, rx, rx0, tok,
-    s_in, s_send, s_xr, s_xe, s_zr, s_sib, s_w, s_kvs, s_kvr, s_ctx, s_rsend, s_rz, s_rr, s_rx, s_out,
+    s_in, s_send, s_xr, s_xf, s_xe, s_zr, s_sib, s_w, s_kvs, s_kvr, s_ctx, s_rsend, s_rz, s_rr, s_rx, s_out,
 ):
     tp, dp = lax.axis_index("tp"), lax.axis_index("dp")
     x, zl, c = tp // 4, (tp // 2) % 2, tp % 2
@@ -65,7 +66,12 @@
         remote(ref, ref, s_w.at[0], sem, sibling).wait_recv()
 
     def cols(q):
+        if q is REST_OF_ROW:
+            return pl.ds(PIECE, THIRD)
         return pl.ds(pl.multiple_of(q * PIECE, PIECE), PIECE)
+
+    def sem_at(q):
+        return 1 if q is REST_OF_ROW else q
 
     def rows(start, size):
         return pl.ds(pl.multiple_of(start, 32), size)
@@ -120,7 +126,7 @@
 
     def send_half(b, q, way):
         ref = half_ref(b, q, way)
-        remote(ref, ref, s_send.at[way, b], s_xr.at[way, b, q], x_ways[way]).start()
+        remote(ref, ref, s_send.at[way, b], s_xf.at[q], x_ways[way]).start()
 
     def send_extra(b, kind, way):
         ref = part_ref(b, 0, kind, c)
@@ -131,33 +137,28 @@
             at = (from_above, from_below)[way]
             dst = xs.at[b, rows(at + c * 32, 32), cols(q)]
             to = (above, below)[way]
-            remote(half_ref(b, q, way), dst, s_send.at[2 + way, b], s_zr.at[way, b, q], to).start()
+            remote(half_ref(b, q, way), dst, s_send.at[2 + way, b], s_zr.at[b, sem_at(q)], to).start()
 
     def send_sib(b, q, kind):
         ref = part_ref(b, q, kind, c)
-        remote(ref, ref, s_send.at[4 + kind, b], s_sib.at[kind, b, q], sibling).start()
+        remote(ref, ref, s_send.at[4 + kind, b], s_sib.at[b, sem_at(q)], sibling).start()
 
     def recv_sib(b, q):
-        for kind in range(3):
-            landed(part_ref(b, q, kind, 1 - c), s_sib.at[kind, b, q])
+        landed(xs.at[b, 0:128, cols(q)], s_sib.at[b, sem_at(q)])
 
     def pass_z(b, q):
-        for way in range(2):
-            landed(part_ref(b, q, 1 + way, c), s_zr.at[way, b, q])
-            send_sib(b, q, 1 + way)
-
-    def start_own(q, carry):
-        send_z(b_own, q)
-
-        @pl.when(q > 0)
-        def _():
-            send_x(b_own, q, 0)
-            send_x(b_own, q, 1)
-
-        send_sib(b_own, q, 0)
-        return carry
-
-    lax.fori_loop(0, NQ, start_own, 0)
+        landed(xs.at[b, 0:64, cols(q)], s_zr.at[b, sem_at(q)])
+        send_sib(b, q, 1)
+        send_sib(b, q, 2)
+
+    send_z(b_own, 0)
+    for q in range(1, NQ):
+        send_x(b_own, q, 0)
+        send_x(b_own, q, 1)
+        if q == 1:
+            send_z(b_own, REST_OF_ROW)
+            send_sib(b_own, 0, 0)
+            send_sib(b_own, REST_OF_ROW, 0)
     in_copies[0].wait()
     in_copies[1].wait()
     wkv_sends = [
@@ -235,29 +236,25 @@
 
     in_copies[2].wait()
 
-    def first_loop(q, carry):
-        @pl.when(q > 0)
-        def _():
-            for b, way in ((b_left, 0), (b_right, 1)):
-                landed(part_ref(b, q, 0, c), s_xr.at[way, b, q])
-                send_z(b, q)
-                send_half(b, q, way)
-                send_sib(b, q, 0)
-
-        pass_z(b_own, q)
-        wo_part(q).start()
-        recv_sib(b_own, q)
-
-        @pl.when(q == 0)
-        def _():
-            other = rows((1 - c) * HD, 64), rows((1 - c) * HD + 64, 64)
-            landed(wkv.at[other[0]], s_w.at[3])
-            landed(wkv.at[other[1]], s_w.at[4])
-
-        qkv(2, b_own, q)
+    def near_piece(q, carry):
+        for b, way in ((b_left, 0), (b_right, 1)):
+            landed(part_ref(b, q, 0, c), s_xr.at[way, b, q])
+            send_z(b, q)
+            send_half(b, q, way)
+            send_sib(b, q, 0)
+        wo_part(q - 1).start()
         return carry
 
-    lax.fori_loop(0, NQ, first_loop, 0)
+    pass_z(b_own, 0)
+    landed(wkv.at[rows((1 - c) * HD, 64)], s_w.at[3])
+    landed(wkv.at[rows((1 - c) * HD + 64, 64)], s_w.at[4])
+    recv_sib(b_own, 0)
+    qkv(2, b_own, 0)
+    lax.fori_loop(1, 3, near_piece, 0)
+    pass_z(b_own, REST_OF_ROW)
+    recv_sib(b_own, REST_OF_ROW)
+    qkv(2, b_own, REST_OF_ROW)
+    lax.fori_loop(3, 4, near_piece, 0)
     for way in range(2):
         send_x(b_own, 0, way)
     for turn in range(2):
@@ -276,23 +273,34 @@
         lax.fori_loop(0, 2, one, 0)
 
     def far_rows(q):
-        for way in range(2):
-            landed(half_ref(b_far, q, way), s_xr.at[way, b_far, q])
+        landed(part_ref(b_far, q, 0, c), s_xf.at[q])
+        send_sib(b_far, q, 0)
+
+    def far_spread(q):
+        far_rows(q)
+        send_z(b_far, q)
 
     def second_loop(i, carry):
         q = i + 1
+
+        @pl.when(i == 1)
+        def _():
+            far_spread(1)
+            far_spread(2)
+
+        @pl.when(i == 2)
+        def _():
+            far_spread(3)
+
         for b in (b_left, b_right):
             pass_z(b, q)
 
         def near(a, b):
             recv_sib(b, q)
-            qkv(a, b, q)
+            qkv_kv(a, b, q)
 
         both(near)
-        far_rows(q)
-        send_z(b_far, q)
-        send_sib(b_far, q, 0)
-        wo_part(4 + i).start()
+        wo_part(3 + i).start()
         return carry
 
     lax.fori_loop(0, NQ - 1, second_loop, 0)
@@ -324,13 +332,13 @@
 
     def near_last(a, b):
         recv_sib(b, 0)
-        qkv(a, b, 0)
-        finish_qkv(a, b)
+        qkv_kv(a, b, 0)
+        finish_kv(a, b)
 
     both(near_last)
+    wo_part(6).start()
     wo_part(7).start()
     far_rows(0)
-    send_sib(b_far, 0, 0)
     for kind in (1, 2):
         landed(part_ref(b_far, 0, kind, c), s_xe.at[kind - 1, b_far])
         send_sib(b_far, 0, kind)
@@ -519,13 +527,19 @@
     drain(b_left, 0)
 
     def near_project(a, b):
-        attend(b)
-
         def sums(q, carry):
             far_sum(q)
             return carry
 
-        lax.fori_loop(1 + a, 2 + 2 * a, sums, 0)
+        def late_q(q, carry):
+            qkv_q(a, b, q)
+            return carry
+
+        lax.fori_loop(0, NQ, late_q, 0)
+        finish_q(a, b)
+        lax.fori_loop(3, 3 + a, sums, 0)
+        attend(b)
+        lax.fori_loop(1, 2 - a, sums, 0)
         ctx_send(b).wait_recv()
 
         def piece(q, carry):
@@ -537,6 +551,7 @@
         project(b, 0)
         for way in range(2):
             pl.when(a == way)(lambda way=way: near_sum_first(way))
+        lax.fori_loop(2, 3 - a, sums, 0)
         lax.fori_loop(2, NQ, piece, 0)
 
     both(near_project)
@@ -645,9 +660,10 @@
             dma((7,)),
             dma((9, NX)),
             dma((2, NX, NQ)),
+            dma((NQ,)),
             dma((2, NX)),
-            dma((2, NX, NQ)),
-            dma((3, NX, NQ)),
+            dma((NX, NQ)),
+            dma((NX, NQ)),
             dma((6,)),
             dma((2, NX)),
             dma((2, NX)),
@@ -674,7 +690,7 @@
         out_shape=(shape, shape),
         in_specs=[block, pl.BlockSpec((1, D), lambda i: (0, 0))],
         out_specs=(block, block),
-        compiler_params=pltpu.CompilerParams(vmem_limit_bytes=60 * 2**20),
+        compiler_params=pltpu.CompilerParams(vmem_limit_bytes=8 * 2**20),
         cost_estimate=pl.CostEstimate(flops=3_000_000, bytes_accessed=3_000_000, transcendentals=64),
     )(stream, gain_mlp)
 

time: 128 us -> 122 us (0.953)
  Pallas kernels: 123 us -> 117 us
    pallas_call x1, Pallas kernels: 119 us -> 115 us  [sublayer(): pl.pallas_call(kernel, out_shape=shape, in_specs=[any_spec, vmem_spec] +...]
    pallas_call x1, Pallas kernels: 3.81 us -> 2.13 us  [sublayer(): pl.pallas_call(final_norm, grid=(4,), out_shape=(shape, shape), in_specs=...]
where the time goes in v4:
time: 122 us; the launch traced here: 121 us
  Pallas kernels  117 us (96%)
  local copies, waits for them, and re-layouts  3.3 us (3%)
    pallas_call x1, Pallas kernels, sublayer(): pl.pallas_call(kernel, out_shape=shape, in_specs=[any_spec, vmem_spec] +...  115 us

profile of v4, /device:TPU:1, one launch (start us, length us, event | category | flops | bytes accessed | tf_op | source)
XLA Modules:
  0.0 120.7 jit_solution(6806427196616046914)
XLA Ops:
  0.6 1.4 %reshape.10.gains = bf16[1,8192]{1,0:T(2,128)(2,1)} reshape(bf16[8192]{0:T(1024)(128)(2,1)} %param.10) | data formatting | bytes 32768 | tf_op jit(solution)/shard_map/reshape | solution.py:630
  2.0 0.7 reshape.11.gain
  2.7 114.6 %shard_map.104.stream_in = bf16[64,8192]{1,0:T(8,128)(2,1)} custom-call(bf16[64,8192]{1,0:T(8,128)(2,1)} %tok_hbm.1, bf16[1,8192]{1,0:T(2,128)(2,1)} %reshape.10.gains, bf16[8192,512]{1,0:T(8,128)(2,1)} %wq_hbm.1, bf16[64,8192]{1,0:T(8,128)(2,1)} %bitcast.2, bf16[64,8192]{1,0:T(8,128)(2,1)} %bitcast.3, bf16[512,8192]{1,0:T(8,128)(2,1)} %wo_hbm.1, ...), custom_call_target="tpu_custom_call" | custom-call | flops 24000000000 | bytes 24000000 | tf_op jit(solution)/shard_map/pallas_call | solution.py:635
  117.4 0.0 copy-start
  117.4 1.2 %copy-done = bf16[64,8192]{1,0:T(8,128)(2,1)S(1)} copy-done((bf16[64,8192]{1,0:T(8,128)(2,1)S(1)}, bf16[64,8192]{1,0:T(8,128)(2,1)}, u32[]{:S(2)}) %copy-start) | copy-done | bytes 1048600
  118.6 2.1 %shard_map.105 = (bf16[64,8192]{1,0:T(8,128)(2,1)}, bf16[64,8192]{1,0:T(8,128)(2,1)}) custom-call(bf16[64,8192]{1,0:T(8,128)(2,1)S(1)} %copy-done, bf16[1,8192]{1,0:T(2,128)(2,1)S(1)} %reshape.11.gain), custom_call_target="tpu_custom_call" | custom-call | flops 3000000 | bytes 3000000 | tf_op jit(solution)/shard_map/pallas_call | solution.py:687
Async XLA Ops:
  117.4 1.2 %copy-start = (bf16[64,8192]{1,0:T(8,128)(2,1)S(1)}, bf16[64,8192]{1,0:T(8,128)(2,1)}, u32[]{:S(2)}) copy-start(bf16[64,8192]{1,0:T(8,128)(2,1)} %shard_map.104.stream_in) | copy-start | bytes 3145732

commit v5 on v4

--- a/solution.py
+++ b/solution.py
@@ -27,6 +27,12 @@
 CHUNK = HEADS * BLK // NCH
 
 
+def scaled(value, gain):
+    factor = gain[...].astype(F32)
+    parts = [value[:, k * HD : (k + 1) * HD] * factor[k : k + 1] for k in range(D // HD)]
+    return jnp.concatenate(parts, axis=1)
+
+
 def rotary_tables():
     inverse = np.exp(np.arange(HD // 2) * (-2.0 * math.log(500000.0) / HD))
     angles = np.arange(NX * BLK)[:, None] * inverse[None, :]
@@ -100,7 +106,7 @@
         part = pl.ds(pl.multiple_of(i * 16, 16), 16)
         as_float = tok[part, :].astype(F32)
         inv = lax.rsqrt(jnp.mean(as_float * as_float, axis=-1, keepdims=True) + 1e-05)
-        normed = as_float * inv * gains[...].astype(F32)
+        normed = scaled(as_float * inv, gains)
         xs[x, pl.ds(pl.multiple_of(c * 64 + i * 16, 16), 16), :] = normed.astype(BF16)
         return carry
 
@@ -242,7 +248,8 @@
             send_z(b, q)
             send_half(b, q, way)
             send_sib(b, q, 0)
-        wo_part(q - 1).start()
+        wo_part(2 * q - 2).start()
+        wo_part(2 * q - 1).start()
         return carry
 
     pass_z(b_own, 0)
@@ -300,7 +307,11 @@
             qkv_kv(a, b, q)
 
         both(near)
-        wo_part(3 + i).start()
+
+        @pl.when(i < 2)
+        def _():
+            wo_part(6 + i).start()
+
         return carry
 
     lax.fori_loop(0, NQ - 1, second_loop, 0)
@@ -323,7 +334,7 @@
             pl.when(i == kind)(lambda kind=kind: near_first(kind))
         pass_z(b_far, i + 1)
         recv_sib(b_far, i + 1)
-        qkv(2, b_far, i + 1)
+        qkv_kv(2, b_far, i + 1)
         return carry
 
     lax.fori_loop(0, NQ - 1, third_loop, 0)
@@ -335,22 +346,29 @@
         qkv_kv(a, b, 0)
         finish_kv(a, b)
 
-    both(near_last)
-    wo_part(6).start()
-    wo_part(7).start()
+    near_last(0, b_right)
     far_rows(0)
+    near_last(1, b_left)
     for kind in (1, 2):
         landed(part_ref(b_far, 0, kind, c), s_xe.at[kind - 1, b_far])
         send_sib(b_far, 0, kind)
     recv_sib(b_far, 0)
     qkv_kv(2, b_far, 0)
     finish_kv(2, b_far)
-    qkv_q(2, b_far, 0)
-    finish_q(2, b_far)
+
+    def all_q(a, b):
+        def one(q, carry):
+            qkv_q(a, b, q)
+            return carry
+
+        lax.fori_loop(0, NQ, one, 0)
+        finish_q(a, b)
+
 
     for b in (b_right, b_left):
         kv_send(b).wait_recv()
         kv_pass(b).start()
+    all_q(2, b_far)
     for b in (b_own, b_right, b_left):
         kv_wait(b)
 
@@ -531,12 +549,7 @@
             far_sum(q)
             return carry
 
-        def late_q(q, carry):
-            qkv_q(a, b, q)
-            return carry
-
-        lax.fori_loop(0, NQ, late_q, 0)
-        finish_q(a, b)
+        all_q(a, b)
         lax.fori_loop(3, 3 + a, sums, 0)
         attend(b)
         lax.fori_loop(1, 2 - a, sums, 0)
@@ -622,12 +635,12 @@
     stream_out[...] = stream
     as_float = stream.astype(F32)
     inv = lax.rsqrt(jnp.mean(as_float * as_float, axis=-1, keepdims=True) + 1e-05)
-    mlp_out[...] = (as_float * inv * gain[...].astype(F32)).astype(BF16)
+    mlp_out[...] = scaled(as_float * inv, gain).astype(BF16)
 
 
 def sublayer(tokens, gain_attn, w_query, w_key, w_value, w_out, gain_mlp):
     cos, sin = rotary_tables()
-    gain_attn, gain_mlp = gain_attn.reshape(1, D), gain_mlp.reshape(1, D)
+    gain_attn, gain_mlp = gain_attn.reshape(D // HD, HD), gain_mlp.reshape(D // HD, HD)
     any_spec = pl.BlockSpec(memory_space=pl.ANY)
     vmem_spec = pl.BlockSpec(memory_space=pltpu.VMEM)
     dma = pltpu.SemaphoreType.DMA
@@ -688,7 +701,7 @@
         final_norm,
         grid=(4,),
         out_shape=(shape, shape),
-        in_specs=[block, pl.BlockSpec((1, D), lambda i: (0, 0))],
+        in_specs=[block, pl.BlockSpec((D // HD, HD), lambda i: (0, 0))],
         out_specs=(block, block),
         compiler_params=pltpu.CompilerParams(vmem_limit_bytes=8 * 2**20),
         cost_estimate=pl.CostEstimate(flops=3_000_000, bytes_accessed=3_000_000, transcendentals=64),

time: 122 us -> 119 us (0.975)
  local copies, waits for them, and re-layouts: 3.3 us -> 1.22 us
    reshape x2 -> x0, local copies, waits for them, and re-layouts: 2.09 us -> none  [sublayer(): gain_attn, gain_mlp = (gain_attn.reshape(1, D), gain_mlp.reshape(1, D))]
where the time goes in v5:
time: 119 us; the launch traced here: 118 us
  Pallas kernels  116 us (97%)
  local copies, waits for them, and re-layouts  1.22 us (1%)
    pallas_call x1, Pallas kernels, sublayer(): pl.pallas_call(kernel, out_shape=shape, in_specs=[any_spec, vmem_spec] +...  114 us

profile of v5, /device:TPU:1, one launch (start us, length us, event | category | flops | bytes accessed | tf_op | source)
XLA Modules:
  0.0 118.2 jit_solution(8541903679224789943)
XLA Ops:
  0.6 0.0 copy-start.1
  0.6 114.2 %shard_map.104.stream_in = bf16[64,8192]{1,0:T(8,128)(2,1)} custom-call(bf16[64,8192]{1,0:T(8,128)(2,1)} %tok_hbm.1, bf16[64,128]{1,0:T(8,128)(2,1)} %bitcast.7, bf16[8192,512]{1,0:T(8,128)(2,1)} %wq_hbm.1, bf16[64,8192]{1,0:T(8,128)(2,1)} %bitcast.5, bf16[64,8192]{1,0:T(8,128)(2,1)} %bitcast.6, bf16[512,8192]{1,0:T(8,128)(2,1)} %wo_hbm.1, ...), custom_call_target="tpu_custom_call" | custom-call | flops 24000000000 | bytes 24000000 | tf_op jit(solution)/shard_map/pallas_call | solution.py:648
  114.9 0.0 copy-done.1
  114.9 0.0 copy-start
  114.9 1.2 %copy-done = bf16[64,8192]{1,0:T(8,128)(2,1)S(1)} copy-done((bf16[64,8192]{1,0:T(8,128)(2,1)S(1)}, bf16[64,8192]{1,0:T(8,128)(2,1)}, u32[]{:S(2)}) %copy-start) | copy-done | bytes 1048600
  116.1 2.1 %shard_map.105 = (bf16[64,8192]{1,0:T(8,128)(2,1)}, bf16[64,8192]{1,0:T(8,128)(2,1)}) custom-call(bf16[64,8192]{1,0:T(8,128)(2,1)S(1)} %copy-done, bf16[64,128]{1,0:T(8,128)(2,1)S(1)} %bitcast.4), custom_call_target="tpu_custom_call" | custom-call | flops 3000000 | bytes 3000000 | tf_op jit(solution)/shard_map/pallas_call | solution.py:700
Async XLA Ops:
  0.6 114.2 %copy-start.1 = (bf16[8192]{0:T(1024)(128)(2,1)S(1)}, bf16[8192]{0:T(1024)(128)(2,1)}, u32[]{:S(2)}) copy-start(bf16[8192]{0:T(1024)(128)(2,1)} %param.15) | copy-start | bytes 49156
  114.9 1.2 %copy-start = (bf16[64,8192]{1,0:T(8,128)(2,1)S(1)}, bf16[64,8192]{1,0:T(8,128)(2,1)}, u32[]{:S(2)}) copy-start(bf16[64,8192]{1,0:T(8,128)(2,1)} %shard_map.104.stream_in) | copy-start | bytes 3145732

commit v6 on v5

--- a/solution.py
+++ b/solution.py
@@ -57,6 +57,7 @@
     right, left = device((x + 1) % 4, zz, c), device((x + 3) % 4, zz, c)
     above, below = device(x, (zz + 1) % 4, c), device(x, (zz + 3) % 4, c)
     across, sibling = device(x, (zz + 2) % 4, c), device(x, zz, 1 - c)
+    opposite = device(x, (zz + 2) % 4, 1 - c)
     b_own, b_right, b_far, b_left = x, (x + 1) % 4, (x + 2) % 4, (x + 3) % 4
 
     def remote(src, dst, send_sem, recv_sem, to):
@@ -85,7 +86,7 @@
     tok_copy = pltpu.make_async_copy(tok_hbm, tok, s_in.at[0])
     tok_copy.start()
     barrier = pltpu.get_barrier_semaphore()
-    for neighbour in (right, left, above, below, across, sibling):
+    for neighbour in (right, left, above, below, across, opposite, sibling):
         pl.semaphore_signal(barrier, inc=1, device_id=neighbour, device_id_type=MESH)
 
     wk_rows, wv_rows = rows(c * HD, 64), rows(c * HD + 64, 64)
@@ -111,7 +112,7 @@
         return carry
 
     lax.fori_loop(0, 4, norm_rows, 0)
-    pl.semaphore_wait(barrier, 6)
+    pl.semaphore_wait(barrier, 7)
 
     from_below = 192 - 64 * zl
     from_above = 128 + 64 * zl
@@ -353,8 +354,12 @@
         landed(part_ref(b_far, 0, kind, c), s_xe.at[kind - 1, b_far])
         send_sib(b_far, 0, kind)
     recv_sib(b_far, 0)
+    kv_both = remote(
+        kvl.at[b_far, c], kvr.at[b_far, c], s_kvs.at[1, b_far], s_kvr.at[1, b_far], opposite
+    )
     qkv_kv(2, b_far, 0)
     finish_kv(2, b_far)
+    kv_both.start()
 
     def all_q(a, b):
         def one(q, carry):
@@ -442,7 +447,6 @@
 
     def far_kv():
         kv_send(b_far).wait_recv()
-        kv_pass(b_far).start()
         kv_wait(b_far)
 
     def third_cols(q):

time: 119 us -> 119 us (level)
  no operation moved by 1% of the time
where the time goes in v6:
time: 119 us; the launch traced here: 118 us
  Pallas kernels  116 us (97%)
  local copies, waits for them, and re-layouts  1.22 us (1%)
    pallas_call x1, Pallas kernels, sublayer(): pl.pallas_call(kernel, out_shape=shape, in_specs=[any_spec, vmem_spec] +...  114 us

profile of v6, /device:TPU:1, one launch (start us, length us, event | category | flops | bytes accessed | tf_op | source)
XLA Modules:
  0.0 117.8 jit_solution(10820802754436312528)
XLA Ops:
  0.6 0.0 copy-start.1
  0.6 113.8 %shard_map.104.stream_in = bf16[64,8192]{1,0:T(8,128)(2,1)} custom-call(bf16[64,8192]{1,0:T(8,128)(2,1)} %tok_hbm.1, bf16[64,128]{1,0:T(8,128)(2,1)} %bitcast.7, bf16[8192,512]{1,0:T(8,128)(2,1)} %wq_hbm.1, bf16[64,8192]{1,0:T(8,128)(2,1)} %bitcast.5, bf16[64,8192]{1,0:T(8,128)(2,1)} %bitcast.6, bf16[512,8192]{1,0:T(8,128)(2,1)} %wo_hbm.1, ...), custom_call_target="tpu_custom_call" | custom-call | flops 24000000000 | bytes 24000000 | tf_op jit(solution)/shard_map/pallas_call | solution.py:652
  114.5 0.0 copy-done.1
  114.5 0.0 copy-start
  114.5 1.2 %copy-done = bf16[64,8192]{1,0:T(8,128)(2,1)S(1)} copy-done((bf16[64,8192]{1,0:T(8,128)(2,1)S(1)}, bf16[64,8192]{1,0:T(8,128)(2,1)}, u32[]{:S(2)}) %copy-start) | copy-done | bytes 1048600
  115.7 2.1 %shard_map.105 = (bf16[64,8192]{1,0:T(8,128)(2,1)}, bf16[64,8192]{1,0:T(8,128)(2,1)}) custom-call(bf16[64,8192]{1,0:T(8,128)(2,1)S(1)} %copy-done, bf16[64,128]{1,0:T(8,128)(2,1)S(1)} %bitcast.4), custom_call_target="tpu_custom_call" | custom-call | flops 3000000 | bytes 3000000 | tf_op jit(solution)/shard_map/pallas_call | solution.py:704
Async XLA Ops:
  0.6 113.8 %copy-start.1 = (bf16[8192]{0:T(1024)(128)(2,1)S(1)}, bf16[8192]{0:T(1024)(128)(2,1)}, u32[]{:S(2)}) copy-start(bf16[8192]{0:T(1024)(128)(2,1)} %param.15) | copy-start | bytes 49156
  114.5 1.2 %copy-start = (bf16[64,8192]{1,0:T(8,128)(2,1)S(1)}, bf16[64,8192]{1,0:T(8,128)(2,1)}, u32[]{:S(2)}) copy-start(bf16[64,8192]{1,0:T(8,128)(2,1)} %shard_map.104.stream_in) | copy-start | bytes 3145732
